TPU v7x, 32 devices: a whole 2x2x4 slice. The times are simulated.
32 devices in a mesh: gx: 4 (over z), gy: 4 (over x, core), gz: 2 (over y).
Axes of the slice: x: 2, y: 2, z: 4, core: 2. Of those that a mesh axis runs over, the one named last changes fastest.
Arguments:
- field: float32 [256, 512, 512], P('gz', 'gx', 'gy'), may hold values from -6 to 6
- peaks: float32 [4], replicated, may hold values from -1.5 to 1.5
- tint: float32 [3], replicated, may hold values from -2 to 2
- light: float32 [3], replicated, may hold values from -1 to 1
Outputs:
- image: float32 [4, 512, 512], P(None, ('gx', 'gz'), 'gy')
All inputs are finite; a program needn't handle non-finite values.
Results may differ from a plain program's by a relative error of at most 0.0003.
Values sent between devices are 32-bit elements; how exact they have to be, the bound alone decides.
No kernel may reach another device: no remote copies, remote signals or barrier semaphores. Data moves between devices by JAX's collectives and lax.ppermute only.
A program may use at most 256 MiB of HBM per device.

v0:
```python
import functools
import math

import jax
import jax.numpy as jnp
from jax import lax
from jax.experimental import pallas as pl
from jax.experimental.pallas import tpu as pltpu
from jax.sharding import PartitionSpec as P

extinction = 1.5
LANES = 128
PAD = 8
HALO = 2
STEP = 16
GROUP = 32
AHEAD = 8
LOG2E = math.log2(math.e)
MIB = 1 << 20
F32 = jnp.float32
BF16 = jnp.bfloat16


def exchanged(first, last, axis):
    count = lax.axis_size(axis)
    forward = [(i, (i + 1) % count) for i in range(count)]
    backward = [(target, source) for source, target in forward]
    return lax.ppermute(last, axis, forward), lax.ppermute(first, axis, backward)


def exchanged_both(both, axis):
    count = lax.axis_size(axis)
    width = both.shape[0] // 2
    if count == 2:
        return lax.ppermute(both, axis, [(0, 1), (1, 0)]), width, 0
    return jnp.concatenate(exchanged(both[:width], both[width:], axis), axis=0), 0, width


def rows_of(shift, count, part):
    return pl.multiple_of(lax.rem(lax.axis_index("gz") + shift, count) * part, 8)


def weigh(peaks, scale, f, optical, before):
    bump = None
    for k in range(peaks.shape[0]):
        gap = f - peaks[k]
        term = jnp.exp2(gap * (gap * (-2.0 * LOG2E)))
        bump = term if bump is None else bump + term
    optical = optical + bump * scale
    after = jnp.exp2(optical)
    return optical, after, before - after


def pack_kernel(field, low, high, x_first, x_last, z_both, cells, totals, sems):
    depth, rows, _ = field.shape
    chunks = depth // STEP

    def fetch(chunk):
        at = pl.ds(chunk * STEP, STEP)
        return pltpu.make_async_copy(field.at[at], cells.at[at], sems.at[chunk])

    for chunk in range(chunks):
        fetch(chunk).start()
    lane = lax.broadcasted_iota(jnp.int32, (rows, LANES), 1)

    def one(block, none):
        offset = 2 + 2 * lax.rem(block, 2)
        group = (lane + (LANES + 2 - offset)) % LANES // 4
        total = jnp.zeros((rows, LANES), F32)
        for half in range(32 // STEP):
            chunk = block * (32 // STEP) + half
            fetch(chunk).wait()
            for step in range(STEP):
                z = chunk * STEP + step
                index = half * STEP + step
                total = jnp.where(group == index, pltpu.roll(cells[z], 4 * index + offset, 1), total)
                x_first[pl.ds(HALO * z, HALO), :] = cells[z, pl.ds(0, HALO), :]
                x_last[pl.ds(HALO * z, HALO), :] = cells[z, pl.ds(rows - HALO, HALO), :]
        totals[block] = total
        return none

    lax.fori_loop(0, depth // 32, one, 0)
    z_both[pl.ds(0, HALO)] = cells[pl.ds(0, HALO)]
    z_both[pl.ds(HALO, HALO)] = cells[pl.ds(depth - HALO, HALO)]
    odd = lane % 4 >= 2
    for block in range(depth // 64):
        one_half, two_half = totals[2 * block], totals[2 * block + 1]
        low[block] = jnp.where(odd, one_half, two_half)
        high[block] = jnp.where(odd, two_half, one_half)


def weight_kernel(scale, count, part, peaks, field, weight, through, cells, optical, sems):
    depth, _, _ = field.shape
    chunks = depth // STEP

    def fetch(turn, chunk):
        at = pl.ds(chunk * STEP, STEP)
        return pltpu.make_async_copy(
            field.at[at, pl.ds(rows_of(turn + 1, count, part), part), :],
            cells.at[at, pl.ds(turn * part, part), :],
            sems.at[turn, chunk],
        )

    for turn in range(count - 1):
        for chunk in range(chunks):
            fetch(turn, chunk).start()
    optical[...] = jnp.zeros_like(optical)
    through[...] = jnp.ones_like(through)
    for turn in range(count - 1):

        def one(chunk, none, turn=turn):
            fetch(turn, chunk).wait()
            depths, passed = optical[turn], through[turn]
            for step in range(STEP):
                z = chunk * STEP + step
                f = cells[z, pl.ds(turn * part, part), :]
                depths, passed, weight[turn, z] = weigh(peaks, scale, f, depths, passed)
            optical[turn], through[turn] = depths, passed
            return none

        lax.fori_loop(0, chunks, one, 0)


def edges(begin, part, low_halo, high_halo, low, high, edge):
    at = pl.ds(begin, part)
    place = lax.broadcasted_iota(jnp.int32, (part, LANES), 1) % 4
    for block in range(low.shape[0]):
        below = low_halo[block, at, :] - high[block, at, :]
        above = high_halo[block, at, :] - low[block, at, :]
        for half in range(2):
            if half == 1:
                below, above = pltpu.roll(below, LANES - 2, 1), pltpu.roll(above, LANES - 2, 1)
            right = jnp.where(place == 1, pltpu.roll(above, LANES - 1, 1), 0.0) - 0.125 * pltpu.roll(above, LANES - 2, 1)
            left = 0.125 * pltpu.roll(below, 2, 1) - jnp.where(place == 2, pltpu.roll(below, 1, 1), 0.0)
            edge[2 * block + half] = jnp.where(place < 2, right, left)


def difference_matrix():
    row = lax.broadcasted_iota(jnp.int32, (2 * LANES, LANES), 0)
    column = lax.broadcasted_iota(jnp.int32, (2 * LANES, LANES), 1)
    ahead = (row - column + 2 * LANES) % LANES
    values = jnp.where(ahead == 1, 1.0, jnp.where(ahead == LANES - 1, -1.0, 0.0))
    values = values + jnp.where(ahead == 2, -0.125, jnp.where(ahead == LANES - 2, 0.125, 0.0))
    return values.astype(BF16)


def shade_kernel(shift, count, part, group, ahead, lower_at, upper_at, scale, peaks, tint, light, field, weight, through,
                 x_low, x_high, z_both, low_halo, high_halo, low, high, out, cells, edge, matrix, slope_a, slope_b, sems):
    depth, rows, _ = field.shape
    chunks = depth // STEP
    begin = rows_of(shift, count, part)
    main = pl.ds(PAD, part)

    def fetch(chunk):
        at = pl.ds(chunk * STEP, STEP)
        into = pl.ds(HALO + chunk * STEP, STEP)
        below = pl.multiple_of(jnp.maximum(begin - PAD, 0), 8)
        above = pl.multiple_of(jnp.minimum(begin + part, rows - PAD), 8)
        return (
            pltpu.make_async_copy(field.at[at, pl.ds(begin, part), :], cells.at[into, main, :], sems.at[0, chunk]),
            pltpu.make_async_copy(field.at[at, pl.ds(below, PAD), :], cells.at[into, pl.ds(0, PAD), :], sems.at[1, chunk]),
            pltpu.make_async_copy(field.at[at, pl.ds(above, PAD), :], cells.at[into, pl.ds(PAD + part, PAD), :], sems.at[2, chunk]),
        )

    for chunk in range(chunks):
        for copy in fetch(chunk):
            copy.start()
    matrix[...] = difference_matrix()
    edges(begin, part, low_halo, high_halo, low, high, edge)
    cells[pl.ds(0, HALO), main, :] = z_both[pl.ds(lower_at, HALO), pl.ds(begin, part), :]
    cells[pl.ds(HALO + depth, HALO), main, :] = z_both[pl.ds(upper_at, HALO), pl.ds(begin, part), :]

    def arrive(chunk):
        for copy in fetch(chunk):
            copy.wait()

        @pl.when(begin == 0)
        def _():
            for step in range(STEP):
                z = chunk * STEP + step
                cells[HALO + z, pl.ds(PAD - HALO, HALO), :] = x_low[pl.ds(HALO * z, HALO), :]

        @pl.when(begin + part == rows)
        def _():
            for step in range(STEP):
                z = chunk * STEP + step
                cells[HALO + z, pl.ds(PAD + part, HALO), :] = x_high[pl.ds(HALO * z, HALO), :]

    arrive(0)
    lane = lax.broadcasted_iota(jnp.int32, (group, LANES), 1)
    rim = (lane < HALO) | (lane >= LANES - HALO)
    for start in range(0, part, group):

        def prepare(first, slopes):
            f = cells[pl.ds(HALO + first, ahead), pl.ds(PAD + start, group), :].reshape(ahead * group, LANES)
            upper = f.astype(BF16)
            lower = (f - upper.astype(F32)).astype(BF16)
            both = jnp.concatenate([upper, lower], axis=1)
            product = jnp.dot(both, matrix[...], preferred_element_type=F32)
            kept = edge[first // 32, pl.ds(start, group), :]
            for step in range(ahead):
                turn = lax.rem(2 * LANES - 2 - 4 * lax.rem(first + step, 32), LANES)
                fix = jnp.where(rim, pltpu.roll(kept, turn, 1), 0.0)
                slopes[step] = product[step * group : (step + 1) * group] + fix

        def use(first, slopes, carry):
            sums, seen = carry[:4], carry[4:]
            for step in range(ahead):
                z = first + step

                def at(dz, dx):
                    return cells[HALO + z + dz, PAD + start + dx : PAD + start + dx + group, :]

                def slope(far_up, up, down, far_down):
                    return (up - down) - 0.125 * (far_up - far_down)

                f = at(0, 0)
                qz = slope(at(2, 0), at(1, 0), at(-1, 0), at(-2, 0))
                qx = slope(at(0, 2), at(0, 1), at(0, -1), at(0, -2))
                qy = slopes[step]
                along = qx * (0.7 * light[0]) + qy * (0.7 * light[1]) + qz * (0.7 * light[2])
                inverse = lax.rsqrt(qx * qx + qy * qy + qz * qz + 2.25)
                if weight is None:
                    optical, passed, own = weigh(peaks, scale, f, *seen)
                    seen = (optical, passed)
                else:
                    own = weight[z, pl.ds(start, group), :]
                lit = own * (0.3 + jnp.abs(along * inverse))
                sums = (sums[0] + lit,) + tuple(
                    sums[c + 1] + lit * jnp.tanh(f * (0.5 * tint[c])) for c in range(3)
                )
            return sums + seen

        def one(chunk, carry):
            if start == 0:

                @pl.when(chunk + 1 < chunks)
                def _():
                    arrive(chunk + 1)

            for part_at in range(0, STEP, 2 * ahead):
                first = chunk * STEP + part_at
                prepare(first + ahead, slope_b)
                carry = use(first, slope_a, carry)
                prepare(jnp.minimum(first + 2 * ahead, depth - ahead), slope_a)
                carry = use(first + ahead, slope_b, carry)
            return carry

        prepare(0, slope_a)
        zero = jnp.zeros((group, LANES), F32)
        seen = (zero, zero + 1.0) if weight is None else ()
        carry = lax.fori_loop(0, chunks, one, (zero,) * 4 + seen)
        for c in range(3):
            out[c, pl.ds(start, group), :] = 0.5 * (carry[0] + carry[c + 1])
        out[3, pl.ds(start, group), :] = carry[5] if weight is None else through[pl.ds(start, group), :]


def fused_kernel(shift, count, part, group, ahead, lower_at, upper_at, scale, peaks, tint, light, field, *rest):
    shade_kernel(shift, count, part, group, ahead, lower_at, upper_at, scale, peaks, tint, light, field, None, None, *rest)


def blend_kernel(count, *refs):
    pieces, image = refs[:-1], refs[-1]
    me = lax.axis_index("gz")
    sources = [lax.rem(me + 2 * count - 1 - k, count) for k in range(count)]
    light = [piece[3] for piece in pieces]
    rgb = [None] * 3
    for k in range(count):
        before = jnp.ones_like(light[0])
        for other in range(count):
            if other != k:
                before = before * jnp.where(sources[other] < sources[k], light[other], 1.0)
        for c in range(3):
            term = before * pieces[k][c]
            rgb[c] = term if rgb[c] is None else rgb[c] + term
    for c in range(3):
        image[c] = rgb[c]
    image[3] = 1.0 - functools.reduce(jnp.multiply, light)


SMEM = pl.BlockSpec(memory_space=pltpu.SMEM)
VMEM = pl.BlockSpec(memory_space=pltpu.VMEM)
HBM = pl.BlockSpec(memory_space=pltpu.HBM)


def cost(cells, flops, terms):
    return pl.CostEstimate(flops=cells * flops, bytes_accessed=cells * 8, transcendentals=cells * terms)


def body(field, peaks, tint, light):
    depth, rows, lanes = field.shape
    count = lax.axis_size("gz")
    part = rows // count
    turns = count - 1
    cells = depth * rows * lanes
    chunks = depth // STEP
    shape = jax.ShapeDtypeStruct
    scale = -extinction / (depth * count) * LOG2E

    def params(mib):
        return pltpu.CompilerParams(vmem_limit_bytes=mib * MIB)

    low, high, x_first, x_last, z_own = pl.pallas_call(
        pack_kernel,
        out_shape=(
            shape((depth // 64, rows, lanes), F32),
            shape((depth // 64, rows, lanes), F32),
            shape((HALO * depth, lanes), F32),
            shape((HALO * depth, lanes), F32),
            shape((2 * HALO, rows, lanes), F32),
        ),
        in_specs=[HBM],
        out_specs=(VMEM,) * 5,
        scratch_shapes=[
            pltpu.VMEM((depth, rows, lanes), F32),
            pltpu.VMEM((depth // 32, rows, lanes), F32),
            pltpu.SemaphoreType.DMA((chunks,)),
        ],
        compiler_params=params(60),
        cost_estimate=cost(cells, 10, 0),
        name="pack",
    )(field)
    x_low, x_high = exchanged(x_first, x_last, "gx")
    z_both, lower_at, upper_at = exchanged_both(z_own, "gz")
    low_halo, high_halo = exchanged(low, high, "gy")

    weights, throughs = pl.pallas_call(
        functools.partial(weight_kernel, scale, count, part),
        out_shape=(pltpu.VMEM((turns, depth, part, lanes), F32), shape((turns, part, lanes), F32)),
        in_specs=[SMEM, HBM],
        out_specs=(VMEM, VMEM),
        scratch_shapes=[
            pltpu.VMEM((depth, turns * part, lanes), F32),
            pltpu.VMEM((turns, part, lanes), F32),
            pltpu.SemaphoreType.DMA((turns, chunks)),
        ],
        compiler_params=params(48),
        cost_estimate=cost(cells * turns // count, 18, 5),
        name="weights",
    )(peaks, field)

    group, ahead = min(GROUP, part), AHEAD
    pieces = []
    for turn in range(count):
        shift = (turn + 1) % count
        own = shift == 0
        operands = [peaks, tint, light, field]
        if not own:
            operands += [weights[turn], throughs[turn]]
        operands += [x_low, x_high, z_both, low_halo, high_halo, low, high]
        piece = pl.pallas_call(
            functools.partial(
                fused_kernel if own else shade_kernel, shift, count, part, group, ahead, lower_at, upper_at, scale
            ),
            out_shape=shape((4, part, lanes), F32),
            in_specs=[SMEM, SMEM, SMEM, HBM] + [VMEM] * (len(operands) - 4),
            out_specs=VMEM,
            scratch_shapes=[
                pltpu.VMEM((depth + 2 * HALO, part + 2 * PAD, lanes), F32),
                pltpu.VMEM((depth // 32, part, lanes), F32),
                pltpu.VMEM((2 * lanes, lanes), BF16),
                pltpu.VMEM((ahead, group, lanes), F32),
                pltpu.VMEM((ahead, group, lanes), F32),
                pltpu.SemaphoreType.DMA((3, chunks)),
            ],
            compiler_params=params(48),
            cost_estimate=cost(cells // count, 40, 4),
            name="fused" if own else "shade",
        )(*operands)
        if not own:
            piece = lax.ppermute(piece, "gz", [(i, (i + shift) % count) for i in range(count)])
        pieces.append(piece)
    return pl.pallas_call(
        functools.partial(blend_kernel, count),
        out_shape=shape((4, part, lanes), F32),
        in_specs=[VMEM] * count,
        out_specs=VMEM,
        name="blend",
    )(*pieces)


def solution(mesh):
    in_specs = (P("gz", "gx", "gy"), P(), P(), P())
    out_specs = P(None, ("gx", "gz"), "gy")
    return jax.shard_map(body, mesh=mesh, in_specs=in_specs, out_specs=out_specs, check_vma=False)
```

profile of v0, /device:TPU:0, one launch (start us, length us, event | category | flops | bytes accessed | tf_op | source)
XLA Modules:
  0.0 44.2 jit_solution(5318805456522858241)
XLA Ops:
  0.0 0.0 copy-start.3
  0.0 0.0 copy-start.4
  0.0 0.0 copy-start.5
  0.0 5.0 %pack.1 = (f32[2,128,128]{2,1,0:T(8,128)}, f32[2,128,128]{2,1,0:T(8,128)}, f32[256,128]{1,0:T(8,128)}, f32[256,128]{1,0:T(8,128)}, f32[4,128,128]{2,1,0:T(8,128)}) custom-call(f32[128,128,128]{2,1,0:T(8,128)} %field.7), custom_call_target="tpu_custom_call" | custom-call | flops 20971520 | bytes 16777216 | tf_op jit(solution)/shard_map/pack/pallas_call | solution.py:303
  5.0 0.0 copy-start
  5.0 0.0 copy-start.1
  5.1 3.0 %collective-permute-start.2 = (f32[4,128,128]{2,1,0:T(8,128)}, f32[4,128,128]{2,1,0:T(8,128)S(1)}, u32[]{:S(2)}, u32[]{:S(2)}) collective-permute-start(f32[4,128,128]{2,1,0:T(8,128)} %get-tuple-element.16), channel_id=1, source_target_pairs={{0,1},{1,0},{2,3},{3,2},{4,5},{5,4},{6,7},{7,6},{8,9},{9,8},{10,11... | collective-permute-start | bytes 786440 | tf_op jit(solution)/shard_map/ppermute | solution.py:35
  8.1 1.6 %collective-permute-start = (f32[256,128]{1,0:T(8,128)}, f32[256,128]{1,0:T(8,128)S(1)}, u32[]{:S(2)}, u32[]{:S(2)}) collective-permute-start(f32[256,128]{1,0:T(8,128)} %get-tuple-element.14), channel_id=1, source_target_pairs={{0,8},{8,16},{16,24},{24,0},{1,9},{9,17},{17,25},{25,1},{2,10},{10... | collective-permute-start | bytes 393224 | tf_op jit(solution)/shard_map/ppermute | solution.py:28
  9.7 2.2 %collective-permute-start.1 = (f32[256,128]{1,0:T(8,128)}, f32[256,128]{1,0:T(8,128)S(1)}, u32[]{:S(2)}, u32[]{:S(2)}) collective-permute-start(f32[256,128]{1,0:T(8,128)} %get-tuple-element.15), channel_id=1, source_target_pairs={{8,0},{16,8},{24,16},{0,24},{9,1},{17,9},{25,17},{1,25},{10,2},{18... | collective-permute-start | bytes 393224 | tf_op jit(solution)/shard_map/ppermute | solution.py:28
  11.9 0.0 collective-permute-start.3
  11.9 1.7 %collective-permute-start.4 = (f32[2,128,128]{2,1,0:T(8,128)}, f32[2,128,128]{2,1,0:T(8,128)S(1)}, u32[]{:S(2)}, u32[]{:S(2)}) collective-permute-start(f32[2,128,128]{2,1,0:T(8,128)} %get-tuple-element.18.low.rest_5_), channel_id=1, source_target_pairs={{2,0},{4,2},{6,4},{0,6},{3,1},{5,3},{7,5},{1,7},{10,8},{12,10},{14... | collective-permute-start | bytes 393224 | tf_op jit(solution)/shard_map/ppermute | solution.py:28
  13.7 0.0 copy-done.3
  13.7 4.9 %weights.1 = (f32[1,128,64,128]{3,2,1,0:T(8,128)S(1)}, f32[1,64,128]{2,1,0:T(8,128)S(1)}) custom-call(f32[4]{0:T(128)S(1)} %copy-done.3, f32[128,128,128]{2,1,0:T(8,128)} %field.7), custom_call_target="tpu_custom_call" | custom-call | flops 18874368 | bytes 8388608 | tf_op jit(solution)/shard_map/weights/pallas_call | solution.py:327
  18.6 0.0 collective-permute-done.x_low.rest_0_
  18.6 0.0 collective-permute-done.1.x_high.rest_1_
  18.6 0.0 collective-permute-done.3.low_halo.rest_3_
  18.6 0.0 collective-permute-done.4.high_halo.rest_4_
  18.6 0.0 collective-permute-done.2.z_both.rest_2_
  18.7 0.0 copy-done.4
  18.7 0.0 copy-done.5
  18.7 0.0 copy-done
  18.7 0.0 copy-done.1
  18.7 9.6 %shade.1 = f32[4,64,128]{2,1,0:T(8,128)S(1)} custom-call(f32[4]{0:T(128)S(1)} %copy-done.3, f32[3]{0:T(128)S(1)} %copy-done.4, f32[3]{0:T(128)S(1)} %copy-done.5, f32[128,128,128]{2,1,0:T(8,128)} %field.7, f32[128,64,128]{2,1,0:T(8,128)S(1)} %bitcast.2, f32[64,128]{1,0:T(8,128)S(1)} %bitcast.3, f32[256,128]{1,0:T(8,128)S(1)} %collective-permute-done.x_low.rest_0_, ...), custom_call_target="tpu_custom_call" | custom-call | flops 41943040 | bytes 8388608 | tf_op jit(solution)/shard_map/shade/pallas_call | solution.py:351
  28.3 0.4 collective-permute-start.5
  28.7 12.6 %fused.1.refs_1_ = f32[4,64,128]{2,1,0:T(8,128)S(1)} custom-call(f32[4]{0:T(128)S(1)} %copy-done.3, f32[3]{0:T(128)S(1)} %copy-done.4, f32[3]{0:T(128)S(1)} %copy-done.5, f32[128,128,128]{2,1,0:T(8,128)} %field.7, f32[256,128]{1,0:T(8,128)S(1)} %collective-permute-done.x_low.rest_0_, f32[256,128]{1,0:T(8,128)S(1)} %collective-permute-done.1.x_high.rest_1_, ...), custom_call_target="tpu_custom_call" | custom-call | flops 41943040 | bytes 8388608 | tf_op jit(solution)/shard_map/fused/pallas_call | solution.py:351
  41.3 0.0 copy-start.2
  41.3 0.6 %copy-done.2 = f32[4,64,128]{2,1,0:T(8,128)} copy-done((f32[4,64,128]{2,1,0:T(8,128)}, f32[4,64,128]{2,1,0:T(8,128)S(1)}, u32[]{:S(2)}) %copy-start.2) | copy-done | bytes 131096
  41.9 0.0 collective-permute-done.5.refs_0_
  41.9 0.0 copy-start.6
  41.9 0.6 %copy-done.6 = f32[4,64,128]{2,1,0:T(8,128)} copy-done((f32[4,64,128]{2,1,0:T(8,128)}, f32[4,64,128]{2,1,0:T(8,128)S(1)}, u32[]{:S(2)}) %copy-start.6) | copy-done | bytes 131096
  42.6 1.6 %blend.1 = f32[4,64,128]{2,1,0:T(8,128)} custom-call(f32[4,64,128]{2,1,0:T(8,128)} %copy-done.6, f32[4,64,128]{2,1,0:T(8,128)} %copy-done.2), custom_call_target="tpu_custom_call" | custom-call | tf_op jit(solution)/shard_map/blend/pallas_call | solution.py:373
Async XLA Ops:
  0.0 13.7 %copy-start.3 = (f32[4]{0:T(128)S(1)}, f32[4]{0:T(128)}, u32[]{:S(2)}) copy-start(f32[4]{0:T(128)} %peaks.5) | copy-start | bytes 52
  0.0 18.7 %copy-start.4 = (f32[3]{0:T(128)S(1)}, f32[3]{0:T(128)}, u32[]{:S(2)}) copy-start(f32[3]{0:T(128)} %tint.3) | copy-start | bytes 40
  0.0 18.7 %copy-start.5 = (f32[3]{0:T(128)S(1)}, f32[3]{0:T(128)}, u32[]{:S(2)}) copy-start(f32[3]{0:T(128)} %light.3) | copy-start | bytes 40
  5.0 13.6 %copy-start = (f32[2,128,128]{2,1,0:T(8,128)S(1)}, f32[2,128,128]{2,1,0:T(8,128)}, u32[]{:S(2)}) copy-start(f32[2,128,128]{2,1,0:T(8,128)} %get-tuple-element.18.low.rest_5_) | copy-start | bytes 393220
  5.0 13.6 %copy-start.1 = (f32[2,128,128]{2,1,0:T(8,128)S(1)}, f32[2,128,128]{2,1,0:T(8,128)}, u32[]{:S(2)}) copy-start(f32[2,128,128]{2,1,0:T(8,128)} %get-tuple-element.17.high.rest_6_) | copy-start | bytes 393220
  5.1 13.6 %collective-permute-start.2 = (f32[4,128,128]{2,1,0:T(8,128)}, f32[4,128,128]{2,1,0:T(8,128)S(1)}, u32[]{:S(2)}, u32[]{:S(2)}) collective-permute-start(f32[4,128,128]{2,1,0:T(8,128)} %get-tuple-element.16), channel_id=1, source_target_pairs={{0,1},{1,0},{2,3},{3,2},{4,5},{5,4},{6,7},{7,6},{8,9},{9,8},{10,11... | collective-permute-start | bytes 786440 | tf_op jit(solution)/shard_map/ppermute | solution.py:35
  8.1 10.5 %collective-permute-start = (f32[256,128]{1,0:T(8,128)}, f32[256,128]{1,0:T(8,128)S(1)}, u32[]{:S(2)}, u32[]{:S(2)}) collective-permute-start(f32[256,128]{1,0:T(8,128)} %get-tuple-element.14), channel_id=1, source_target_pairs={{0,8},{8,16},{16,24},{24,0},{1,9},{9,17},{17,25},{25,1},{2,10},{10... | collective-permute-start | bytes 393224 | tf_op jit(solution)/shard_map/ppermute | solution.py:28
  9.7 8.9 %collective-permute-start.1 = (f32[256,128]{1,0:T(8,128)}, f32[256,128]{1,0:T(8,128)S(1)}, u32[]{:S(2)}, u32[]{:S(2)}) collective-permute-start(f32[256,128]{1,0:T(8,128)} %get-tuple-element.15), channel_id=1, source_target_pairs={{8,0},{16,8},{24,16},{0,24},{9,1},{17,9},{25,17},{1,25},{10,2},{18... | collective-permute-start | bytes 393224 | tf_op jit(solution)/shard_map/ppermute | solution.py:28
  11.9 6.7 %collective-permute-start.3 = (f32[2,128,128]{2,1,0:T(8,128)}, f32[2,128,128]{2,1,0:T(8,128)S(1)}, u32[]{:S(2)}, u32[]{:S(2)}) collective-permute-start(f32[2,128,128]{2,1,0:T(8,128)} %get-tuple-element.17.high.rest_6_), channel_id=1, source_target_pairs={{0,2},{2,4},{4,6},{6,0},{1,3},{3,5},{5,7},{7,1},{8,10},{10,12},{12... | collective-permute-start | bytes 393224 | tf_op jit(solution)/shard_map/ppermute | solution.py:28
  11.9 6.7 %collective-permute-start.4 = (f32[2,128,128]{2,1,0:T(8,128)}, f32[2,128,128]{2,1,0:T(8,128)S(1)}, u32[]{:S(2)}, u32[]{:S(2)}) collective-permute-start(f32[2,128,128]{2,1,0:T(8,128)} %get-tuple-element.18.low.rest_5_), channel_id=1, source_target_pairs={{2,0},{4,2},{6,4},{0,6},{3,1},{5,3},{7,5},{1,7},{10,8},{12,10},{14... | collective-permute-start | bytes 393224 | tf_op jit(solution)/shard_map/ppermute | solution.py:28
  28.3 13.6 %collective-permute-start.5 = (f32[4,64,128]{2,1,0:T(8,128)S(1)}, f32[4,64,128]{2,1,0:T(8,128)S(1)}, u32[]{:S(2)}, u32[]{:S(2)}) collective-permute-start(f32[4,64,128]{2,1,0:T(8,128)S(1)} %shade.1), channel_id=1, source_target_pairs={{0,1},{1,0},{2,3},{3,2},{4,5},{5,4},{6,7},{7,6},{8,9},{9,8},{10,11... | collective-permute-start | bytes 393224 | tf_op jit(solution)/shard_map/ppermute | solution.py:371
  41.3 0.7 %copy-start.2 = (f32[4,64,128]{2,1,0:T(8,128)}, f32[4,64,128]{2,1,0:T(8,128)S(1)}, u32[]{:S(2)}) copy-start(f32[4,64,128]{2,1,0:T(8,128)S(1)} %fused.1.refs_1_) | copy-start | bytes 393220
  41.9 0.7 %copy-start.6 = (f32[4,64,128]{2,1,0:T(8,128)}, f32[4,64,128]{2,1,0:T(8,128)S(1)}, u32[]{:S(2)}) copy-start(f32[4,64,128]{2,1,0:T(8,128)S(1)} %collective-permute-done.5.refs_0_) | copy-start | bytes 393220
where the time goes:
time: 44.3 us; the launch traced here: 44.2 us
  Pallas kernels  33.8 us (76%)
  starting transfers between devices  8.97 us (20%)
  local copies, waits for them, and re-layouts  1.31 us (3%)
    pallas_call x2, Pallas kernels, body(): pl.pallas_call(functools.partial(fused_kernel if own else shade_kernel, s...  22.2 us
    pallas_call x1, Pallas kernels, body(): pl.pallas_call(pack_kernel, out_shape=(shape((depth // 64, rows, lanes),...  5.02 us
    pallas_call x1, Pallas kernels, body(): pl.pallas_call(functools.partial(weight_kernel, scale, count, part), out_...  4.93 us
    ppermute x2, starting transfers between devices, exchanged(): lax.ppermute(first, axis, backward)  3.99 us
    ppermute x1, starting transfers between devices, exchanged_both(): return (lax.ppermute(both, axis, [(0, 1), (1, 0)]), width, 0)  3.03 us
    pallas_call x1, Pallas kernels, body(): pl.pallas_call(functools.partial(blend_kernel, count), out_shape=shape((4...  1.64 us
    ppermute x2, starting transfers between devices, exchanged(): lax.ppermute(last, axis, forward)  1.58 us
    unnamed x14, local copies, waits for them, and re-layouts  1.31 us
  transfers between devices with their start and end apart: 6, of which 0 were waited for; matrix products, arithmetic and copies ran while one was open for 0% of the time, Pallas kernels for 40%

commit v1 on v0

v1 whole, which is shorter than its diff:
```python
import functools
import math

import jax
import jax.numpy as jnp
from jax import lax
from jax.experimental import pallas as pl
from jax.experimental.pallas import tpu as pltpu
from jax.sharding import PartitionSpec as P

extinction = 1.5
LANES = 128
PAD = 8
HALO = 2
STEP = 16
UNROLL = 16
GROUP = 64
AHEAD = 2
SLOTS = 4
WEIGHT_MIB = 44
SHADE_MIB = 36
FUSED_MIB = 48
LOG2E = math.log2(math.e)
MIB = 1 << 20
F32 = jnp.float32
BF16 = jnp.bfloat16


def exchanged(first, last, axis):
    count = lax.axis_size(axis)
    forward = [(i, (i + 1) % count) for i in range(count)]
    backward = [(target, source) for source, target in forward]
    return lax.ppermute(last, axis, forward), lax.ppermute(first, axis, backward)


def exchanged_both(both, axis):
    count = lax.axis_size(axis)
    width = both.shape[0] // 2
    if count == 2:
        return lax.ppermute(both, axis, [(0, 1), (1, 0)]), width, 0
    return jnp.concatenate(exchanged(both[:width], both[width:], axis), axis=0), 0, width


def rows_of(shift, count, part):
    return pl.multiple_of(lax.rem(lax.axis_index("gz") + shift, count) * part, 8)


def weigh(peaks, scale, f, optical, before):
    bump = None
    for k in range(peaks.shape[0]):
        gap = f - peaks[k]
        term = jnp.exp2(gap * (gap * (-2.0 * LOG2E)))
        bump = term if bump is None else bump + term
    optical = optical + bump * scale
    after = jnp.exp2(optical)
    return optical, after, before - after


def pack_kernel(field, low, high, x_first, x_last, z_both, cells, totals, sems):
    depth, rows, _ = field.shape
    chunks = depth // STEP

    def fetch(chunk):
        at = pl.ds(chunk * STEP, STEP)
        return pltpu.make_async_copy(field.at[at], cells.at[at], sems.at[chunk])

    for chunk in range(chunks):
        fetch(chunk).start()
    lane = lax.broadcasted_iota(jnp.int32, (rows, LANES), 1)

    def one(block, none):
        offset = 2 + 2 * lax.rem(block, 2)
        group = (lane + (LANES + 2 - offset)) % LANES // 4
        total = jnp.zeros((rows, LANES), F32)
        for half in range(32 // STEP):
            chunk = block * (32 // STEP) + half
            fetch(chunk).wait()
            for step in range(STEP):
                z = chunk * STEP + step
                index = half * STEP + step
                total = jnp.where(group == index, pltpu.roll(cells[z], 4 * index + offset, 1), total)
                x_first[pl.ds(HALO * z, HALO), :] = cells[z, pl.ds(0, HALO), :]
                x_last[pl.ds(HALO * z, HALO), :] = cells[z, pl.ds(rows - HALO, HALO), :]
        totals[block] = total
        return none

    lax.fori_loop(0, depth // 32, one, 0)
    for face in (x_first, x_last):
        face[pl.ds(HALO * depth, PAD), :] = jnp.zeros((PAD, LANES), F32)
    z_both[pl.ds(0, HALO)] = cells[pl.ds(0, HALO)]
    z_both[pl.ds(HALO, HALO)] = cells[pl.ds(depth - HALO, HALO)]
    odd = lane % 4 >= 2
    for block in range(depth // 64):
        one_half, two_half = totals[2 * block], totals[2 * block + 1]
        low[block] = jnp.where(odd, one_half, two_half)
        high[block] = jnp.where(odd, two_half, one_half)


def fetches(shift, count, part, field, cells, sems):
    _, rows, _ = field.shape
    begin = rows_of(shift, count, part)
    below = pl.multiple_of(jnp.maximum(begin - PAD, 0), 8)
    above = pl.multiple_of(jnp.minimum(begin + part, rows - PAD), 8)

    def fetch(chunk):
        at = pl.ds(chunk * STEP, STEP)
        into = pl.ds(HALO + chunk * STEP, STEP)
        return (
            pltpu.make_async_copy(field.at[at, pl.ds(begin, part), :], cells.at[into, pl.ds(PAD, part), :], sems.at[0, chunk]),
            pltpu.make_async_copy(field.at[at, pl.ds(below, PAD), :], cells.at[into, pl.ds(0, PAD), :], sems.at[1, chunk]),
            pltpu.make_async_copy(field.at[at, pl.ds(above, PAD), :], cells.at[into, pl.ds(PAD + part, PAD), :], sems.at[2, chunk]),
        )

    return fetch


def weight_kernel(scale, shift, count, part, peaks, field, weight, through, cells, optical, sems):
    depth, _, _ = field.shape
    chunks = depth // STEP
    fetch = fetches(shift, count, part, field, cells, sems)
    for chunk in range(chunks):
        for copy in fetch(chunk):
            copy.start()
    optical[...] = jnp.zeros_like(optical)
    through[...] = jnp.ones_like(through)

    def one(chunk, none):
        for ahead in range(1):
            for copy in fetch(chunk + ahead):
                copy.wait()
        depths, passed = optical[...], through[...]
        for step in range(STEP):
            z = chunk * STEP + step
            depths, passed, weight[z] = weigh(peaks, scale, cells[HALO + z, pl.ds(PAD, part), :], depths, passed)
        optical[...], through[...] = depths, passed
        return none

    lax.fori_loop(0, chunks, one, 0)


def split(f):
    upper = f.astype(BF16)
    return upper, (f - upper.astype(F32)).astype(BF16)


def edges(begin, part, low_halo, high_halo, low, high, edge):
    at = pl.ds(begin, part)
    place = lax.broadcasted_iota(jnp.int32, (part, LANES), 1) % 4
    for block in range(low.shape[0]):
        below = low_halo[block, at, :] - high[block, at, :]
        above = high_halo[block, at, :] - low[block, at, :]
        for half in range(2):
            if half == 1:
                below, above = pltpu.roll(below, LANES - 2, 1), pltpu.roll(above, LANES - 2, 1)
            right = jnp.where(place == 1, pltpu.roll(above, LANES - 1, 1), 0.0) - 0.125 * pltpu.roll(above, LANES - 2, 1)
            left = 0.125 * pltpu.roll(below, 2, 1) - jnp.where(place == 2, pltpu.roll(below, 1, 1), 0.0)
            edge[2 * block + half] = jnp.where(place < 2, right, left)


def slope_of(ahead):
    near = jnp.where(ahead == 1, 1.0, jnp.where(ahead == -1, -1.0, 0.0))
    return near + jnp.where(ahead == 2, -0.125, jnp.where(ahead == -2, 0.125, 0.0))


def lane_matrix():
    row = lax.broadcasted_iota(jnp.int32, (2 * LANES, LANES), 0)
    column = lax.broadcasted_iota(jnp.int32, (2 * LANES, LANES), 1)
    return slope_of((row - column + 2 * LANES + LANES // 2) % LANES - LANES // 2).astype(BF16)


def row_matrix(group):
    window = group + 2 * PAD
    row = lax.broadcasted_iota(jnp.int32, (group, window), 0)
    column = lax.broadcasted_iota(jnp.int32, (group, window), 1)
    slope = slope_of(column - PAD - row)
    return jnp.concatenate([slope, slope], axis=1).astype(BF16)


def shade_kernel(ready, shift, count, part, group, lower_at, upper_at, scale, peaks, tint, light, *refs):
    if ready:
        _, weight, through, *refs = refs
        (x_low, x_high, z_both, low_halo, high_halo, low, high, out, cells, edge, lanes, across, slopes) = refs
        depth = weight.shape[0]
    else:
        field, *refs = refs
        (x_low, x_high, z_both, low_halo, high_halo, low, high, out, cells, edge, lanes, across, slopes, sems) = refs
        depth = field.shape[0]
        fetch = fetches(shift, count, part, field, cells, sems)
    rows = z_both.shape[1]
    chunks = depth // STEP
    turns = depth // UNROLL
    begin = rows_of(shift, count, part)
    main = pl.ds(PAD, part)
    window = group + 2 * PAD

    if not ready:
        for chunk in range(chunks):
            for copy in fetch(chunk):
                copy.start()
    lanes[...] = lane_matrix()
    across[...] = row_matrix(group)
    edges(begin, part, low_halo, high_halo, low, high, edge)
    cells[pl.ds(0, HALO), main, :] = z_both[pl.ds(lower_at, HALO), pl.ds(begin, part), :]
    cells[pl.ds(HALO + depth, HALO), main, :] = z_both[pl.ds(upper_at, HALO), pl.ds(begin, part), :]

    def arrive(chunk, number):
        if not ready:
            for ahead in range(number):
                for copy in fetch(chunk + ahead):
                    copy.wait()

        @pl.when(begin == 0)
        def _():
            for step in range(number * STEP):
                z = chunk * STEP + step
                cells[HALO + z, pl.ds(PAD - HALO, HALO), :] = x_low[pl.ds(HALO * z, HALO), :]

        @pl.when(begin + part == rows)
        def _():
            for step in range(number * STEP):
                z = chunk * STEP + step
                cells[HALO + z, pl.ds(PAD + part, HALO), :] = x_high[pl.ds(HALO * z, HALO), :]

    arrive(0, UNROLL // STEP)
    lane = lax.broadcasted_iota(jnp.int32, (group, LANES), 1)
    rim = (lane < HALO) | (lane >= LANES - HALO)
    for start in range(0, part, group):

        def prepare(first, place):
            kept = edge[first // 32, pl.ds(start, group), :]
            halves = [split(cells[HALO + first + step, pl.ds(start, window), :]) for step in range(2)]
            rows_in = jnp.concatenate([jnp.concatenate(half, axis=1) for half in halves], axis=0)
            along_y = jnp.dot(rows_in, lanes[...], preferred_element_type=F32)
            both = [jnp.concatenate([halves[0][k], halves[1][k]], axis=1) for k in range(2)]
            along_x = jnp.dot(across[...], jnp.concatenate(both, axis=0), preferred_element_type=F32)
            for step in range(2):
                turn = lax.rem(2 * LANES - 2 - 4 * lax.rem(first + step, 32), LANES)
                fix = jnp.where(rim, pltpu.roll(kept, turn, 1), 0.0)
                slopes[(place + step) % SLOTS, 0] = along_x[:, step * LANES : (step + 1) * LANES]
                slopes[(place + step) % SLOTS, 1] = along_y[step * window + PAD : step * window + PAD + group] + fix

        def use(z, place, carry):
            sums, seen = carry[:4], carry[4:]

            def at(dz):
                return cells[HALO + z + dz, pl.ds(PAD + start, group), :]

            f = at(0)
            qx, qy = slopes[place % SLOTS, 0], slopes[place % SLOTS, 1]
            qz = (at(1) - at(-1)) - 0.125 * (at(2) - at(-2))
            along = qx * (0.7 * light[0]) + qy * (0.7 * light[1]) + qz * (0.7 * light[2])
            inverse = lax.rsqrt(qx * qx + qy * qy + qz * qz + 2.25)
            if ready:
                own = weight[z, pl.ds(start, group), :]
            else:
                optical, passed, own = weigh(peaks, scale, f, *seen)
                seen = (optical, passed)
            lit = own * (0.3 + jnp.abs(along * inverse))
            return (sums[0] + lit,) + tuple(sums[c + 1] + lit * jnp.tanh(f * (0.5 * tint[c])) for c in range(3)) + seen

        def one(turn, carry):
            if start == 0:

                @pl.when(turn + 1 < turns)
                def _():
                    arrive((turn + 1) * (UNROLL // STEP), UNROLL // STEP)

            for step in range(0, UNROLL, 2):
                z = turn * UNROLL + step
                later = z + AHEAD
                if step + AHEAD >= UNROLL:
                    later = jnp.minimum(later, depth - 4 + (AHEAD + step) % 4)
                prepare(later, step + AHEAD)
                carry = use(z, step, carry)
                carry = use(z + 1, step + 1, carry)
            return carry

        for step in range(0, AHEAD, 2):
            prepare(step, step)
        zero = jnp.zeros((group, LANES), F32)
        carry = lax.fori_loop(0, turns, one, (zero,) * 4 + (() if ready else (zero, zero + 1.0)))
        for c in range(3):
            out[c, pl.ds(start, group), :] = 0.5 * (carry[0] + carry[c + 1])
        out[3, pl.ds(start, group), :] = through[pl.ds(start, group), :] if ready else carry[5]


SMEM = pl.BlockSpec(memory_space=pltpu.SMEM)
VMEM = pl.BlockSpec(memory_space=pltpu.VMEM)
HBM = pl.BlockSpec(memory_space=pltpu.HBM)


def cost(cells, flops, terms):
    return pl.CostEstimate(flops=cells * flops, bytes_accessed=cells * 8, transcendentals=cells * terms)


def body(field, peaks, tint, light):
    depth, rows, lanes = field.shape
    count = lax.axis_size("gz")
    part = rows // count
    cells = depth * rows * lanes
    chunks = depth // STEP
    shape = jax.ShapeDtypeStruct
    scale = -extinction / (depth * count) * LOG2E

    def params(mib):
        return pltpu.CompilerParams(vmem_limit_bytes=mib * MIB)

    low, high, x_first, x_last, z_own = pl.pallas_call(
        pack_kernel,
        out_shape=(
            shape((depth // 64, rows, lanes), F32),
            shape((depth // 64, rows, lanes), F32),
            shape((HALO * depth + PAD, lanes), F32),
            shape((HALO * depth + PAD, lanes), F32),
            shape((2 * HALO, rows, lanes), F32),
        ),
        in_specs=[HBM],
        out_specs=(VMEM,) * 5,
        scratch_shapes=[
            pltpu.VMEM((depth, rows, lanes), F32),
            pltpu.VMEM((depth // 32, rows, lanes), F32),
            pltpu.SemaphoreType.DMA((chunks,)),
        ],
        compiler_params=params(48),
        cost_estimate=cost(cells, 10, 0),
        name="pack",
    )(field)
    x_low, x_high = exchanged(x_first, x_last, "gx")
    z_both, lower_at, upper_at = exchanged_both(z_own, "gz")
    low_halo, high_halo = exchanged(low, high, "gy")

    group = min(GROUP, part)
    padded = (depth + 2 * HALO, part + 2 * PAD, lanes)
    weight, through, ready_cells = pl.pallas_call(
        functools.partial(weight_kernel, scale, 1, count, part),
        out_shape=(pltpu.VMEM((depth, part, lanes), F32), shape((part, lanes), F32), pltpu.VMEM(padded, F32)),
        in_specs=[SMEM, HBM],
        out_specs=(VMEM, VMEM, VMEM),
        scratch_shapes=[pltpu.VMEM((part, lanes), F32), pltpu.SemaphoreType.DMA((3, chunks))],
        compiler_params=params(WEIGHT_MIB),
        cost_estimate=cost(cells // count, 18, 5),
        name="weights",
    )(peaks, field)

    pieces = []
    for turn in range(count):
        shift = (turn + 1) % count
        ready = turn == 0
        operands = [peaks, tint, light] + ([ready_cells, weight, through] if ready else [field])
        kinds = [SMEM] * 3 + ([VMEM] * 3 if ready else [HBM])
        halos = [x_low, x_high, z_both, low_halo, high_halo, low, high]
        scratch = [
            pltpu.VMEM((depth // 32, part, lanes), F32),
            pltpu.VMEM((2 * lanes, lanes), BF16),
            pltpu.VMEM((group, 2 * (group + 2 * PAD)), BF16),
            pltpu.VMEM((SLOTS, 2, group, lanes), F32),
        ]
        result = shape((4, part, lanes), F32)
        if not ready:
            scratch = [pltpu.VMEM(padded, F32)] + scratch + [pltpu.SemaphoreType.DMA((3, chunks))]
        piece = pl.pallas_call(
            functools.partial(shade_kernel, ready, shift, count, part, group, lower_at, upper_at, scale),
            out_shape=(result, pltpu.VMEM(padded, F32)) if ready else result,
            in_specs=kinds + [VMEM] * len(halos),
            out_specs=(VMEM, VMEM) if ready else VMEM,
            scratch_shapes=scratch,
            input_output_aliases={3: 1} if ready else {},
            compiler_params=params(SHADE_MIB if ready else FUSED_MIB),
            cost_estimate=cost(cells // count, 40, 4),
            name="shade" if ready else "fused",
        )(*operands, *halos)
        if ready:
            piece = piece[0]
        if shift:
            piece = lax.ppermute(piece, "gz", [(i, (i + shift) % count) for i in range(count)])
        pieces.append((lax.rem(lax.axis_index("gz") + count - shift, count), piece))

    image = 0.0
    for source, piece in pieces:
        for other, rest in pieces:
            if other is not source:
                piece = piece * jnp.where(other < source, rest[3:], 1.0)
        image = image + piece
    total = functools.reduce(jnp.multiply, [piece[3:] for _, piece in pieces])
    channel = lax.broadcasted_iota(jnp.int32, image.shape, 0)
    return jnp.where(channel < 3, image, 1.0 - total)


def solution(mesh):
    in_specs = (P("gz", "gx", "gy"), P(), P(), P())
    out_specs = P(None, ("gx", "gz"), "gy")
    return jax.shard_map(body, mesh=mesh, in_specs=in_specs, out_specs=out_specs, check_vma=False)
```

time: 44.3 us -> 39.1 us (0.88)
  Pallas kernels: 33.8 us -> 29.1 us
  local copies, waits for them, and re-layouts: 1.31 us -> 0.02 us
  other arithmetic: 0 us -> 0.75 us
    pallas_call x4 -> x3, Pallas kernels: 28.8 us -> 24.9 us  [the longest x2 19.8 us: body(): pl.pallas_call(functools.partial(shade_kernel, ready, shift, count, part,...]
    unnamed x14 -> x6, local copies, waits for them, and re-layouts: 1.31 us -> 0.02 us
    pallas_call x1, Pallas kernels: 5.02 us -> 4.17 us  [body(): pl.pallas_call(pack_kernel, out_shape=(shape((depth // 64, rows, lanes),...]
    select_n x0 -> x1, other arithmetic: none -> 0.74 us  [body(): return jnp.where(channel < 3, image, 1.0 - total)]
  transfers between devices with their start and end apart: 6 -> 6, of which waited for: 0 -> 0; matrix products, arithmetic and copies ran while one was open for 0% -> 0% of each run, Pallas kernels for 40% -> 44%
where the time goes in v1:
time: 39.1 us; the launch traced here: 38.9 us
  Pallas kernels  29.1 us (74%)
  starting transfers between devices  8.96 us (23%)
  other arithmetic  0.75 us (2%)
    pallas_call x2, Pallas kernels, body(): pl.pallas_call(functools.partial(shade_kernel, ready, shift, count, part,...  19.8 us
    pallas_call x1, Pallas kernels, body(): pl.pallas_call(functools.partial(weight_kernel, scale, 1, count, part), o...  5.1 us
    pallas_call x1, Pallas kernels, body(): pl.pallas_call(pack_kernel, out_shape=(shape((depth // 64, rows, lanes),...  4.17 us
    ppermute x2, starting transfers between devices, exchanged(): lax.ppermute(first, axis, backward)  3.99 us
    ppermute x1, starting transfers between devices, exchanged_both(): return (lax.ppermute(both, axis, [(0, 1), (1, 0)]), width, 0)  3.03 us
    ppermute x2, starting transfers between devices, exchanged(): lax.ppermute(last, axis, forward)  1.58 us
  transfers between devices with their start and end apart: 6, of which 0 were waited for; matrix products, arithmetic and copies ran while one was open for 0% of the time, Pallas kernels for 44%

profile of v1, /device:TPU:0, one launch (start us, length us, event | category | flops | bytes accessed | tf_op | source)
XLA Modules:
  0.0 38.9 jit_solution(1234210440947126161)
XLA Ops:
  0.0 0.0 copy-start
  0.0 4.2 %pack.1 = (f32[2,128,128]{2,1,0:T(8,128)S(1)}, f32[2,128,128]{2,1,0:T(8,128)S(1)}, f32[264,128]{1,0:T(8,128)S(1)}, f32[264,128]{1,0:T(8,128)S(1)}, f32[4,128,128]{2,1,0:T(8,128)S(1)}) custom-call(f32[128,128,128]{2,1,0:T(8,128)} %refs_0_.1), custom_call_target="tpu_custom_call" | custom-call | flops 20971520 | bytes 16777216 | tf_op jit(solution)/shard_map/pack/pallas_call | solution.py:308
  4.2 0.0 copy-start.1
  4.2 0.0 copy-start.2
  4.2 3.0 %collective-permute-start.2 = (f32[4,128,128]{2,1,0:T(8,128)S(1)}, f32[4,128,128]{2,1,0:T(8,128)S(1)}, u32[]{:S(2)}, u32[]{:S(2)}) collective-permute-start(f32[4,128,128]{2,1,0:T(8,128)S(1)} %get-tuple-element.19), channel_id=1, source_target_pairs={{0,1},{1,0},{2,3},{3,2},{4,5},{5,4},{6,7},{7,6},{8,9},{9,8},{10,11... | collective-permute-start | bytes 786440 | tf_op jit(solution)/shard_map/ppermute | solution.py:40
  7.2 1.6 %collective-permute-start = (f32[264,128]{1,0:T(8,128)S(1)}, f32[264,128]{1,0:T(8,128)S(1)}, u32[]{:S(2)}, u32[]{:S(2)}) collective-permute-start(f32[264,128]{1,0:T(8,128)S(1)} %get-tuple-element.17), channel_id=1, source_target_pairs={{0,8},{8,16},{16,24},{24,0},{1,9},{9,17},{17,25},{25,1},{2,10},{10... | collective-permute-start | bytes 405512 | tf_op jit(solution)/shard_map/ppermute | solution.py:33
  8.8 2.2 %collective-permute-start.1 = (f32[264,128]{1,0:T(8,128)S(1)}, f32[264,128]{1,0:T(8,128)S(1)}, u32[]{:S(2)}, u32[]{:S(2)}) collective-permute-start(f32[264,128]{1,0:T(8,128)S(1)} %get-tuple-element.18), channel_id=1, source_target_pairs={{8,0},{16,8},{24,16},{0,24},{9,1},{17,9},{25,17},{1,25},{10,2},{18... | collective-permute-start | bytes 405512 | tf_op jit(solution)/shard_map/ppermute | solution.py:33
  11.1 0.0 collective-permute-start.3
  11.1 1.7 %collective-permute-start.4 = (f32[2,128,128]{2,1,0:T(8,128)S(1)}, f32[2,128,128]{2,1,0:T(8,128)S(1)}, u32[]{:S(2)}, u32[]{:S(2)}) collective-permute-start(f32[2,128,128]{2,1,0:T(8,128)S(1)} %get-tuple-element.21.refs_8_.refs_6_), channel_id=1, source_target_pairs={{2,0},{4,2},{6,4},{0,6},{3,1},{5,3},{7,5},{1,7},{10,8},{12,10},{14... | collective-permute-start | bytes 393224 | tf_op jit(solution)/shard_map/ppermute | solution.py:33
  12.8 0.0 copy-done
  12.8 5.1 %weights.1 = (f32[128,64,128]{2,1,0:T(8,128)S(1)}, f32[64,128]{1,0:T(8,128)S(1)}, f32[132,80,128]{2,1,0:T(8,128)S(1)}) custom-call(f32[4]{0:T(128)S(1)} %copy-done, f32[128,128,128]{2,1,0:T(8,128)} %refs_0_.1), custom_call_target="tpu_custom_call" | custom-call | flops 18874368 | bytes 8388608 | tf_op jit(solution)/shard_map/weights/pallas_call | solution.py:334
  17.9 0.0 collective-permute-done.3.refs_6_.refs_4_
  17.9 0.0 collective-permute-done.4.refs_7_.refs_5_
  17.9 0.0 collective-permute-done.refs_3_.refs_1_
  17.9 0.0 collective-permute-done.1.refs_4_.refs_2_
  18.0 0.0 collective-permute-done.2.refs_5_.refs_3_
  18.0 0.0 copy-done.1
  18.0 0.0 copy-done.2
  18.0 8.0 %shade.1 = (f32[4,64,128]{2,1,0:T(8,128)S(1)}, f32[132,80,128]{2,1,0:T(8,128)S(1)}) custom-call(f32[4]{0:T(128)S(1)} %copy-done, f32[3]{0:T(128)S(1)} %copy-done.1, f32[3]{0:T(128)S(1)} %copy-done.2, f32[132,80,128]{2,1,0:T(8,128)S(1)} %get-tuple-element.14.refs_0_, f32[128,64,128]{2,1,0:T(8,128)S(1)} %get-tuple-element.15.refs_1_, ...), custom_call_target="tpu_custom_call", output_to_operand_aliasing={{1}: (3, {})} | custom-call | flops 41943040 | bytes 8388608 | tf_op jit(solution)/shard_map/shade/pallas_call | solution.py:361
  26.0 0.4 collective-permute-start.5
  26.3 11.8 %fused.1 = f32[4,64,128]{2,1,0:T(8,128)S(1)} custom-call(f32[4]{0:T(128)S(1)} %copy-done, f32[3]{0:T(128)S(1)} %copy-done.1, f32[3]{0:T(128)S(1)} %copy-done.2, f32[128,128,128]{2,1,0:T(8,128)} %refs_0_.1, f32[264,128]{1,0:T(8,128)S(1)} %collective-permute-done.refs_3_.refs_1_, f32[264,128]{1,0:T(8,128)S(1)} %collective-permute-done.1.refs_4_.refs_2_, ...), custom_call_target="tpu_custom_call" | custom-call | flops 41943040 | bytes 8388608 | tf_op jit(solution)/shard_map/fused/pallas_call | solution.py:361
  38.2 0.0 collective-permute-done.5
  38.2 0.7 %add_select_fusion = f32[4,64,128]{2,1,0:T(8,128)} fusion(f32[4,64,128]{2,1,0:T(8,128)S(1)} %fused.1, f32[4,64,128]{2,1,0:T(8,128)S(1)} %collective-permute-done.5, f32[64,128]{1,0:T(8,128)S(1)} %get-tuple-element.24, f32[64,128]{1,0:T(8,128)S(1)} %get-tuple-element.25, f32[64,128]{1,0:T(8,128)S(1)} %get-tuple-element.23, pred[4]{0:T(512)(128)(4,1)S(1)} %iota_compare_fusion), kind=kLoop, calls=%fused_computation | loop fusion | flops 131072 | bytes 491524 | tf_op jit(solution)/shard_map/jit(_where)/select_n | solution.py:386
  (2 shorter events, 0.0 us)
Async XLA Ops:
  0.0 12.8 %copy-start = (f32[4]{0:T(128)S(1)}, f32[4]{0:T(128)}, u32[]{:S(2)}) copy-start(f32[4]{0:T(128)} %peaks.5) | copy-start | bytes 52
  4.2 13.8 %copy-start.1 = (f32[3]{0:T(128)S(1)}, f32[3]{0:T(128)}, u32[]{:S(2)}) copy-start(f32[3]{0:T(128)} %tint.3) | copy-start | bytes 40
  4.2 13.8 %copy-start.2 = (f32[3]{0:T(128)S(1)}, f32[3]{0:T(128)}, u32[]{:S(2)}) copy-start(f32[3]{0:T(128)} %light.3) | copy-start | bytes 40
  4.2 13.8 %collective-permute-start.2 = (f32[4,128,128]{2,1,0:T(8,128)S(1)}, f32[4,128,128]{2,1,0:T(8,128)S(1)}, u32[]{:S(2)}, u32[]{:S(2)}) collective-permute-start(f32[4,128,128]{2,1,0:T(8,128)S(1)} %get-tuple-element.19), channel_id=1, source_target_pairs={{0,1},{1,0},{2,3},{3,2},{4,5},{5,4},{6,7},{7,6},{8,9},{9,8},{10,11... | collective-permute-start | bytes 786440 | tf_op jit(solution)/shard_map/ppermute | solution.py:40
  7.2 10.7 %collective-permute-start = (f32[264,128]{1,0:T(8,128)S(1)}, f32[264,128]{1,0:T(8,128)S(1)}, u32[]{:S(2)}, u32[]{:S(2)}) collective-permute-start(f32[264,128]{1,0:T(8,128)S(1)} %get-tuple-element.17), channel_id=1, source_target_pairs={{0,8},{8,16},{16,24},{24,0},{1,9},{9,17},{17,25},{25,1},{2,10},{10... | collective-permute-start | bytes 405512 | tf_op jit(solution)/shard_map/ppermute | solution.py:33
  8.8 9.1 %collective-permute-start.1 = (f32[264,128]{1,0:T(8,128)S(1)}, f32[264,128]{1,0:T(8,128)S(1)}, u32[]{:S(2)}, u32[]{:S(2)}) collective-permute-start(f32[264,128]{1,0:T(8,128)S(1)} %get-tuple-element.18), channel_id=1, source_target_pairs={{8,0},{16,8},{24,16},{0,24},{9,1},{17,9},{25,17},{1,25},{10,2},{18... | collective-permute-start | bytes 405512 | tf_op jit(solution)/shard_map/ppermute | solution.py:33
  11.1 6.9 %collective-permute-start.3 = (f32[2,128,128]{2,1,0:T(8,128)S(1)}, f32[2,128,128]{2,1,0:T(8,128)S(1)}, u32[]{:S(2)}, u32[]{:S(2)}) collective-permute-start(f32[2,128,128]{2,1,0:T(8,128)S(1)} %get-tuple-element.20.refs_9_.refs_7_), channel_id=1, source_target_pairs={{0,2},{2,4},{4,6},{6,0},{1,3},{3,5},{5,7},{7,1},{8,10},{10,12},{12... | collective-permute-start | bytes 393224 | tf_op jit(solution)/shard_map/ppermute | solution.py:33
  11.1 6.9 %collective-permute-start.4 = (f32[2,128,128]{2,1,0:T(8,128)S(1)}, f32[2,128,128]{2,1,0:T(8,128)S(1)}, u32[]{:S(2)}, u32[]{:S(2)}) collective-permute-start(f32[2,128,128]{2,1,0:T(8,128)S(1)} %get-tuple-element.21.refs_8_.refs_6_), channel_id=1, source_target_pairs={{2,0},{4,2},{6,4},{0,6},{3,1},{5,3},{7,5},{1,7},{10,8},{12,10},{14... | collective-permute-start | bytes 393224 | tf_op jit(solution)/shard_map/ppermute | solution.py:33
  26.0 12.2 %collective-permute-start.5 = (f32[4,64,128]{2,1,0:T(8,128)S(1)}, f32[4,64,128]{2,1,0:T(8,128)S(1)}, u32[]{:S(2)}, u32[]{:S(2)}) collective-permute-start(f32[4,64,128]{2,1,0:T(8,128)S(1)} %get-tuple-element.22), channel_id=1, source_target_pairs={{0,1},{1,0},{2,3},{3,2},{4,5},{5,4},{6,7},{7,6},{8,9},{9,8},{10,11... | collective-permute-start | bytes 393224 | tf_op jit(solution)/shard_map/ppermute | solution.py:375

commit v2 on v1

v2 whole, which is shorter than its diff:
```python
import functools
import math

import jax
import jax.numpy as jnp
from jax import lax
from jax.experimental import pallas as pl
from jax.experimental.pallas import tpu as pltpu
from jax.sharding import PartitionSpec as P

extinction = 1.5
LANES = 128
PAD = 8
HALO = 2
STEP = 16
UNROLL = 32
GROUP = 64
AHEAD = 4
SLOTS = 8
QUAD = 4
WEIGHT_MIB = 24
SHADE_MIB = 24
FUSED_MIB = 48
LOG2E = math.log2(math.e)
MIB = 1 << 20
F32 = jnp.float32
BF16 = jnp.bfloat16


def exchanged(first, last, axis):
    count = lax.axis_size(axis)
    forward = [(i, (i + 1) % count) for i in range(count)]
    backward = [(target, source) for source, target in forward]
    return lax.ppermute(last, axis, forward), lax.ppermute(first, axis, backward)


def exchanged_both(both, axis):
    count = lax.axis_size(axis)
    width = both.shape[0] // 2
    if count == 2:
        return lax.ppermute(both, axis, [(0, 1), (1, 0)]), width, 0
    return jnp.concatenate(exchanged(both[:width], both[width:], axis), axis=0), 0, width


def rows_of(shift, count, part):
    return pl.multiple_of(lax.rem(lax.axis_index("gz") + shift, count) * part, 8)


def weigh(peaks, scale, f, optical, before):
    bump = None
    for k in range(peaks.shape[0]):
        gap = f - peaks[k]
        term = jnp.exp2(gap * (gap * (-2.0 * LOG2E)))
        bump = term if bump is None else bump + term
    optical = optical + bump * scale
    after = jnp.exp2(optical)
    return optical, after, before - after


def pack_kernel(field, low, high, x_first, x_last, z_both, cells, totals, sems):
    depth, rows, _ = field.shape
    chunks = depth // STEP

    def fetch(chunk):
        into = cells.at[pl.ds(HALO + chunk * STEP, STEP), pl.ds(PAD, rows), :]
        return pltpu.make_async_copy(field.at[pl.ds(chunk * STEP, STEP)], into, sems.at[chunk])

    for chunk in range(chunks):
        fetch(chunk).start()
    lane = lax.broadcasted_iota(jnp.int32, (rows, LANES), 1)

    def one(block, none):
        offset = 2 + 2 * lax.rem(block, 2)
        group = (lane + (LANES + 2 - offset)) % LANES // 4
        total = jnp.zeros((rows, LANES), F32)
        for half in range(32 // STEP):
            chunk = block * (32 // STEP) + half
            fetch(chunk).wait()
            for step in range(STEP):
                z = chunk * STEP + step
                index = half * STEP + step
                total = jnp.where(group == index, pltpu.roll(cells[HALO + z, pl.ds(PAD, rows), :], 4 * index + offset, 1), total)
                x_first[pl.ds(HALO * z, HALO), :] = cells[HALO + z, pl.ds(PAD, HALO), :]
                x_last[pl.ds(HALO * z, HALO), :] = cells[HALO + z, pl.ds(PAD + rows - HALO, HALO), :]
        totals[block] = total
        return none

    lax.fori_loop(0, depth // 32, one, 0)
    for face in (x_first, x_last):
        face[pl.ds(HALO * depth, PAD), :] = jnp.zeros((PAD, LANES), F32)
    z_both[pl.ds(0, HALO)] = cells[pl.ds(HALO, HALO), pl.ds(PAD, rows), :]
    z_both[pl.ds(HALO, HALO)] = cells[pl.ds(depth, HALO), pl.ds(PAD, rows), :]
    odd = lane % 4 >= 2
    for block in range(depth // 64):
        one_half, two_half = totals[2 * block], totals[2 * block + 1]
        low[block] = jnp.where(odd, one_half, two_half)
        high[block] = jnp.where(odd, two_half, one_half)


def weight_kernel(scale, shift, count, part, peaks, cells, weight, through, optical):
    depth = weight.shape[0]
    at = pl.ds(pl.multiple_of(rows_of(shift, count, part) + PAD, 8), part)
    optical[...] = jnp.zeros_like(optical)
    through[...] = jnp.ones_like(through)

    def one(turn, none):
        depths, passed = optical[...], through[...]
        for step in range(UNROLL):
            z = turn * UNROLL + step
            depths, passed, weight[z] = weigh(peaks, scale, cells[HALO + z, at, :], depths, passed)
        optical[...], through[...] = depths, passed
        return none

    lax.fori_loop(0, depth // UNROLL, one, 0)


def split(f):
    upper = f.astype(BF16)
    return upper, (f - upper.astype(F32)).astype(BF16)


def edges(begin, part, low_halo, high_halo, low, high, edge):
    at = pl.ds(begin, part)
    place = lax.broadcasted_iota(jnp.int32, (part, LANES), 1) % 4
    for block in range(low.shape[0]):
        below = low_halo[block, at, :] - high[block, at, :]
        above = high_halo[block, at, :] - low[block, at, :]
        for half in range(2):
            if half == 1:
                below, above = pltpu.roll(below, LANES - 2, 1), pltpu.roll(above, LANES - 2, 1)
            right = jnp.where(place == 1, pltpu.roll(above, LANES - 1, 1), 0.0) - 0.125 * pltpu.roll(above, LANES - 2, 1)
            left = 0.125 * pltpu.roll(below, 2, 1) - jnp.where(place == 2, pltpu.roll(below, 1, 1), 0.0)
            edge[2 * block + half] = jnp.where(place < 2, right, left)


def slope_of(ahead):
    near = jnp.where(ahead == 1, 1.0, jnp.where(ahead == -1, -1.0, 0.0))
    return near + jnp.where(ahead == 2, -0.125, jnp.where(ahead == -2, 0.125, 0.0))


def lane_matrix():
    row = lax.broadcasted_iota(jnp.int32, (2 * LANES, LANES), 0)
    column = lax.broadcasted_iota(jnp.int32, (2 * LANES, LANES), 1)
    return slope_of((row - column + 2 * LANES + LANES // 2) % LANES - LANES // 2).astype(BF16)


def row_matrix(group):
    width = group + 2 * PAD
    row = lax.broadcasted_iota(jnp.int32, (group, width), 0)
    column = lax.broadcasted_iota(jnp.int32, (group, width), 1)
    cell = jnp.where(column < group, column, jnp.where(column < group + PAD, column - group - PAD, column - PAD))
    slope = slope_of(cell - row)
    return jnp.concatenate([slope, slope], axis=1).astype(BF16)


def shade_kernel(shift, count, part, group, lower_at, upper_at, scale, peaks, tint, light, *refs):
    cells, weight, through, *refs = refs
    x_low, x_high, z_both, low_halo, high_halo, low, high, out, edge, lanes, across, slopes, strips = refs
    depth, rows = cells.shape[0] - 2 * HALO, low.shape[1]
    turns = depth // UNROLL
    begin = rows_of(shift, count, part)
    lowest, highest = begin == 0, begin + part == rows

    def beside(turn, none):
        for step in range(UNROLL):
            plane = cells.at[HALO + turn * UNROLL + step]
            below, above = plane[pl.ds(begin, PAD), :], plane[pl.ds(pl.multiple_of(begin + PAD + part, 8), PAD), :]
            strips[turn * UNROLL + step, pl.ds(0, PAD), :] = jnp.where(lowest, 0.0, below)
            strips[turn * UNROLL + step, pl.ds(PAD, PAD), :] = jnp.where(highest, 0.0, above)
        return none

    def beside_halo(turn, none, row, halo):
        for step in range(UNROLL):
            z = turn * UNROLL + step
            strips[z, pl.ds(row, HALO), :] = halo[pl.ds(HALO * z, HALO), :]
        return none

    lax.fori_loop(0, turns, beside, 0)

    @pl.when(lowest)
    def _():
        lax.fori_loop(0, turns, functools.partial(beside_halo, row=PAD - HALO, halo=x_low), 0)

    @pl.when(highest)
    def _():
        lax.fori_loop(0, turns, functools.partial(beside_halo, row=PAD, halo=x_high), 0)

    lanes[...] = lane_matrix()
    across[...] = row_matrix(group)
    edges(begin, part, low_halo, high_halo, low, high, edge)
    lane = lax.broadcasted_iota(jnp.int32, (group, LANES), 1)
    rim = (lane < HALO) | (lane >= LANES - HALO)
    for start in range(0, part, group):
        row = pl.multiple_of(begin + start, 8)

        def halved(first, number):
            inner, outer = [], []
            for step in range(number):
                plane = cells.at[HALO + first + step]
                inner.append(split(plane[pl.ds(pl.multiple_of(row + PAD, 8), group), :]))
                below = strips[first + step, pl.ds(0, PAD), :] if start == 0 else plane[pl.ds(row, PAD), :]
                if start + group == part:
                    above = strips[first + step, pl.ds(PAD, PAD), :]
                else:
                    above = plane[pl.ds(pl.multiple_of(row + PAD + group, 8), PAD), :]
                outer.append(split(jnp.concatenate([below, above], axis=0)))
            return inner, outer

        def prepare(first, place):
            kept = edge[first // 32, pl.ds(start, group), :]
            halves, sides = halved(first, QUAD)
            rows_in = jnp.concatenate([jnp.concatenate(half, axis=1) for half in halves], axis=0)
            along_y = jnp.dot(rows_in, lanes[...], preferred_element_type=F32)[:, :LANES]
            for step in range(QUAD):
                turn = lax.rem(2 * LANES - 2 - 4 * lax.rem(first + step, 32), LANES)
                fix = jnp.where(rim, pltpu.roll(kept, turn, 1), 0.0)
                slopes[(place + step) % SLOTS, 1] = along_y[step * group : (step + 1) * group] + fix
            for pair in range(0, QUAD, 2):
                both = [
                    jnp.concatenate([rows[pair][k], rows[pair + 1][k]], axis=1) for k in range(2) for rows in (halves, sides)
                ]
                along_x = jnp.dot(across[...], jnp.concatenate(both, axis=0), preferred_element_type=F32)
                for step in range(2):
                    slopes[(place + pair + step) % SLOTS, 0] = along_x[:, step * LANES : (step + 1) * LANES]

        def use(turn, step, carry):
            z, place = turn * UNROLL + step, step
            sums = carry

            def at(dz):
                layer = cells[HALO + z + dz, pl.ds(pl.multiple_of(row + PAD, 8), group), :]
                if step + dz < 0:
                    layer = jnp.where(turn == 0, z_both[lower_at + HALO + step + dz, pl.ds(row, group), :], layer)
                if step + dz >= UNROLL:
                    beyond = z_both[upper_at + step + dz - UNROLL, pl.ds(row, group), :]
                    layer = jnp.where(turn == turns - 1, beyond, layer)
                return layer

            f = at(0)
            qx, qy = slopes[place % SLOTS, 0], slopes[place % SLOTS, 1]
            qz = (at(1) - at(-1)) - 0.125 * (at(2) - at(-2))
            along = qx * (0.7 * light[0]) + qy * (0.7 * light[1]) + qz * (0.7 * light[2])
            inverse = lax.rsqrt(qx * qx + qy * qy + qz * qz + 2.25)
            own = weight[z, pl.ds(start, group), :]
            lit = own * (0.3 + jnp.abs(along * inverse))
            return (sums[0] + lit,) + tuple(sums[c + 1] + lit * jnp.tanh(f * (0.5 * tint[c])) for c in range(3))

        def one(turn, carry):
            for step in range(0, UNROLL, QUAD):
                z = turn * UNROLL + step
                later = z + AHEAD
                if step + AHEAD >= UNROLL:
                    later = jnp.minimum(later, depth - QUAD)
                prepare(later, step + AHEAD)
                for near in range(QUAD):
                    carry = use(turn, step + near, carry)
            return carry

        for step in range(0, AHEAD, QUAD):
            prepare(step, step)
        zero = jnp.zeros((group, LANES), F32)
        carry = lax.fori_loop(0, turns, one, (zero,) * 4)
        for c in range(3):
            out[c, pl.ds(start, group), :] = 0.5 * (carry[0] + carry[c + 1])
        out[3, pl.ds(start, group), :] = through[pl.ds(start, group), :]


def fetches(shift, count, part, field, cells, sems):
    _, rows, _ = field.shape
    begin = rows_of(shift, count, part)
    below = pl.multiple_of(jnp.maximum(begin - PAD, 0), 8)
    above = pl.multiple_of(jnp.minimum(begin + part, rows - PAD), 8)

    def fetch(chunk):
        at = pl.ds(chunk * STEP, STEP)
        into = pl.ds(HALO + chunk * STEP, STEP)
        return (
            pltpu.make_async_copy(field.at[at, pl.ds(begin, part), :], cells.at[into, pl.ds(PAD, part), :], sems.at[0, chunk]),
            pltpu.make_async_copy(field.at[at, pl.ds(below, PAD), :], cells.at[into, pl.ds(0, PAD), :], sems.at[1, chunk]),
            pltpu.make_async_copy(field.at[at, pl.ds(above, PAD), :], cells.at[into, pl.ds(PAD + part, PAD), :], sems.at[2, chunk]),
        )

    return fetch


def fused_kernel(shift, count, part, group, lower_at, upper_at, scale, peaks, tint, light, *refs):
    field, *refs = refs
    x_low, x_high, z_both, low_halo, high_halo, low, high, out, cells, edge, lanes, across, slopes, sems = refs
    depth = field.shape[0]
    fetch = fetches(shift, count, part, field, cells, sems)
    rows = z_both.shape[1]
    chunks = depth // STEP
    turns = depth // UNROLL
    begin = rows_of(shift, count, part)
    main = pl.ds(PAD, part)

    for chunk in range(chunks):
        for copy in fetch(chunk):
            copy.start()
    lanes[...] = lane_matrix()
    across[...] = row_matrix(group)
    edges(begin, part, low_halo, high_halo, low, high, edge)
    cells[pl.ds(0, HALO), main, :] = z_both[pl.ds(lower_at, HALO), pl.ds(begin, part), :]
    cells[pl.ds(HALO + depth, HALO), main, :] = z_both[pl.ds(upper_at, HALO), pl.ds(begin, part), :]

    def beside(first, number):
        @pl.when(begin == 0)
        def _():
            for step in range(number):
                cells[HALO + first + step, pl.ds(PAD - HALO, HALO), :] = x_low[pl.ds(HALO * (first + step), HALO), :]

        @pl.when(begin + part == rows)
        def _():
            for step in range(number):
                cells[HALO + first + step, pl.ds(PAD + part, HALO), :] = x_high[pl.ds(HALO * (first + step), HALO), :]

    def arrive(chunk, number):
        for ahead in range(number):
            for copy in fetch(chunk + ahead):
                copy.wait()
        beside(chunk * STEP, number * STEP)

    arrive(0, 1)
    lane = lax.broadcasted_iota(jnp.int32, (group, LANES), 1)
    rim = (lane < HALO) | (lane >= LANES - HALO)
    for start in range(0, part, group):

        def halved(first, number):
            inner, outer = [], []
            for step in range(number):
                plane = cells.at[HALO + first + step]
                inner.append(split(plane[pl.ds(PAD + start, group), :]))
                below, above = plane[pl.ds(start, PAD), :], plane[pl.ds(PAD + start + group, PAD), :]
                outer.append(split(jnp.concatenate([below, above], axis=0)))
            return inner, outer

        def prepare(first, place):
            kept = edge[first // 32, pl.ds(start, group), :]
            halves, sides = halved(first, QUAD)
            rows_in = jnp.concatenate([jnp.concatenate(half, axis=1) for half in halves], axis=0)
            along_y = jnp.dot(rows_in, lanes[...], preferred_element_type=F32)[:, :LANES]
            for step in range(QUAD):
                turn = lax.rem(2 * LANES - 2 - 4 * lax.rem(first + step, 32), LANES)
                fix = jnp.where(rim, pltpu.roll(kept, turn, 1), 0.0)
                slopes[(place + step) % SLOTS, 1] = along_y[step * group : (step + 1) * group] + fix
            for pair in range(0, QUAD, 2):
                both = [
                    jnp.concatenate([rows[pair][k], rows[pair + 1][k]], axis=1) for k in range(2) for rows in (halves, sides)
                ]
                along_x = jnp.dot(across[...], jnp.concatenate(both, axis=0), preferred_element_type=F32)
                for step in range(2):
                    slopes[(place + pair + step) % SLOTS, 0] = along_x[:, step * LANES : (step + 1) * LANES]

        def use(z, place, carry):
            sums, seen = carry[:4], carry[4:]

            def at(dz):
                return cells[HALO + z + dz, pl.ds(PAD + start, group), :]

            f = at(0)
            qx, qy = slopes[place % SLOTS, 0], slopes[place % SLOTS, 1]
            qz = (at(1) - at(-1)) - 0.125 * (at(2) - at(-2))
            along = qx * (0.7 * light[0]) + qy * (0.7 * light[1]) + qz * (0.7 * light[2])
            inverse = lax.rsqrt(qx * qx + qy * qy + qz * qz + 2.25)
            optical, passed, own = weigh(peaks, scale, f, *seen)
            seen = (optical, passed)
            lit = own * (0.3 + jnp.abs(along * inverse))
            return (sums[0] + lit,) + tuple(sums[c + 1] + lit * jnp.tanh(f * (0.5 * tint[c])) for c in range(3)) + seen

        def one(turn, carry):
            if start == 0:
                chunk = turn * (UNROLL // STEP) + 1

                @pl.when(turn + 1 < turns)
                def _():
                    arrive(chunk, UNROLL // STEP)

                @pl.when(turn + 1 == turns)
                def _():
                    arrive(chunk, UNROLL // STEP - 1)

            for step in range(0, UNROLL, QUAD):
                z = turn * UNROLL + step
                later = z + AHEAD
                if step + AHEAD >= UNROLL:
                    later = jnp.minimum(later, depth - QUAD)
                prepare(later, step + AHEAD)
                for near in range(QUAD):
                    carry = use(z + near, step + near, carry)
            return carry

        for step in range(0, AHEAD, QUAD):
            prepare(step, step)
        zero = jnp.zeros((group, LANES), F32)
        carry = lax.fori_loop(0, turns, one, (zero,) * 5 + (zero + 1.0,))
        for c in range(3):
            out[c, pl.ds(start, group), :] = 0.5 * (carry[0] + carry[c + 1])
        out[3, pl.ds(start, group), :] = carry[5]


SMEM = pl.BlockSpec(memory_space=pltpu.SMEM)
VMEM = pl.BlockSpec(memory_space=pltpu.VMEM)
HBM = pl.BlockSpec(memory_space=pltpu.HBM)


def cost(cells, flops, terms):
    return pl.CostEstimate(flops=cells * flops, bytes_accessed=cells * 8, transcendentals=cells * terms)


def body(field, peaks, tint, light):
    depth, rows, lanes = field.shape
    count = lax.axis_size("gz")
    part = rows // count
    cells = depth * rows * lanes
    chunks = depth // STEP
    shape = jax.ShapeDtypeStruct
    scale = -extinction / (depth * count) * LOG2E

    def params(mib):
        return pltpu.CompilerParams(vmem_limit_bytes=mib * MIB)

    padded = (depth + 2 * HALO, rows + 2 * PAD, lanes)
    low, high, x_first, x_last, z_own, cells_in = pl.pallas_call(
        pack_kernel,
        out_shape=(
            shape((depth // 64, rows, lanes), F32),
            shape((depth // 64, rows, lanes), F32),
            shape((HALO * depth + PAD, lanes), F32),
            shape((HALO * depth + PAD, lanes), F32),
            shape((2 * HALO, rows, lanes), F32),
            pltpu.VMEM(padded, F32),
        ),
        in_specs=[HBM],
        out_specs=(VMEM,) * 6,
        scratch_shapes=[
            pltpu.VMEM((depth // 32, rows, lanes), F32),
            pltpu.SemaphoreType.DMA((chunks,)),
        ],
        compiler_params=params(48),
        cost_estimate=cost(cells, 10, 0),
        name="pack",
    )(field)
    x_low, x_high = exchanged(x_first, x_last, "gx")
    z_both, lower_at, upper_at = exchanged_both(z_own, "gz")
    low_halo, high_halo = exchanged(low, high, "gy")

    group = min(GROUP, part)
    weight, through = pl.pallas_call(
        functools.partial(weight_kernel, scale, 1, count, part),
        out_shape=(pltpu.VMEM((depth, part, lanes), F32), shape((part, lanes), F32)),
        in_specs=[SMEM, VMEM],
        out_specs=(VMEM, VMEM),
        scratch_shapes=[pltpu.VMEM((part, lanes), F32)],
        compiler_params=params(WEIGHT_MIB),
        cost_estimate=cost(cells // count, 18, 5),
        name="weights",
    )(peaks, cells_in)

    pieces = []
    for turn in range(count):
        shift = (turn + 1) % count
        ready = turn == 0
        operands = [peaks, tint, light] + ([cells_in, weight, through] if ready else [field])
        halos = [x_low, x_high, z_both, low_halo, high_halo, low, high]
        scratch = [
            pltpu.VMEM((depth // 32, part, lanes), F32),
            pltpu.VMEM((2 * lanes, lanes), BF16),
            pltpu.VMEM((group, 2 * (group + 2 * PAD)), BF16),
            pltpu.VMEM((SLOTS, 2, group, lanes), F32),
        ]
        if ready:
            scratch.append(pltpu.VMEM((depth, 2 * PAD, lanes), F32))
        else:
            own_cells = pltpu.VMEM((depth + 2 * HALO, part + 2 * PAD, lanes), F32)
            scratch = [own_cells] + scratch + [pltpu.SemaphoreType.DMA((3, chunks))]
        result = shape((4, part, lanes), F32)
        piece = pl.pallas_call(
            functools.partial(shade_kernel if ready else fused_kernel, shift, count, part, group, lower_at, upper_at, scale),
            out_shape=result,
            in_specs=[SMEM] * 3 + ([VMEM] * 3 if ready else [HBM]) + [VMEM] * len(halos),
            out_specs=VMEM,
            scratch_shapes=scratch,
            compiler_params=params(SHADE_MIB if ready else FUSED_MIB),
            cost_estimate=cost(cells // count, 40, 4),
            name="shade" if ready else "fused",
        )(*operands, *halos)
        if shift:
            piece = lax.ppermute(piece, "gz", [(i, (i + shift) % count) for i in range(count)])
        pieces.append((lax.rem(lax.axis_index("gz") + count - shift, count), piece))

    image = 0.0
    for source, piece in pieces:
        for other, rest in pieces:
            if other is not source:
                piece = piece * jnp.where(other < source, rest[3:], 1.0)
        image = image + piece
    total = functools.reduce(jnp.multiply, [piece[3:] for _, piece in pieces])
    channel = lax.broadcasted_iota(jnp.int32, image.shape, 0)
    return jnp.where(channel < 3, image, 1.0 - total)


def solution(mesh):
    in_specs = (P("gz", "gx", "gy"), P(), P(), P())
    out_specs = P(None, ("gx", "gz"), "gy")
    return jax.shard_map(body, mesh=mesh, in_specs=in_specs, out_specs=out_specs, check_vma=False)
```

time: 39.1 us -> 37.8 us (0.967)
  Pallas kernels: 29.1 us -> 27.5 us
    pallas_call x1, Pallas kernels: 5.1 us -> 3.74 us  [body(): pl.pallas_call(functools.partial(weight_kernel, scale, 1, count, part), o...]
    pallas_call x2, Pallas kernels: 19.8 us -> 18.8 us  [body(): pl.pallas_call(functools.partial(shade_kernel if ready else fused_kernel,...]
    pallas_call x1, Pallas kernels: 4.17 us -> 5.03 us  [body(): pl.pallas_call(pack_kernel, out_shape=(shape((depth // 64, rows, lanes),...]
  transfers between devices with their start and end apart: 6 -> 6, of which waited for: 0 -> 1; matrix products, arithmetic and copies ran while one was open for 0% -> 0% of each run, Pallas kernels for 44% -> 41%
where the time goes in v2:
time: 37.8 us; the launch traced here: 37.7 us
  Pallas kernels  27.5 us (73%)
  starting transfers between devices  9.17 us (24%)
  other arithmetic  0.75 us (2%)
    pallas_call x2, Pallas kernels, body(): pl.pallas_call(functools.partial(shade_kernel if ready else fused_kernel,...  18.8 us
    pallas_call x1, Pallas kernels, body(): pl.pallas_call(pack_kernel, out_shape=(shape((depth // 64, rows, lanes),...  5.03 us
    ppermute x2, starting transfers between devices, exchanged(): lax.ppermute(first, axis, backward)  3.99 us
    pallas_call x1, Pallas kernels, body(): pl.pallas_call(functools.partial(weight_kernel, scale, 1, count, part), o...  3.74 us
    ppermute x1, starting transfers between devices, exchanged_both(): return (lax.ppermute(both, axis, [(0, 1), (1, 0)]), width, 0)  3.03 us
    ppermute x2, starting transfers between devices, exchanged(): lax.ppermute(last, axis, forward)  1.58 us
  transfers between devices with their start and end apart: 6, of which 1 were waited for; matrix products, arithmetic and copies ran while one was open for 0% of the time, Pallas kernels for 41%

profile of v2, /device:TPU:0, one launch (start us, length us, event | category | flops | bytes accessed | tf_op | source)
XLA Modules:
  0.0 37.7 jit_solution(6959909850248131811)
XLA Ops:
  0.0 0.0 copy-start.2
  0.0 0.0 copy-start.3
  0.0 0.0 copy-start.4
  0.0 5.0 %pack.1 = (f32[2,128,128]{2,1,0:T(8,128)}, f32[2,128,128]{2,1,0:T(8,128)}, f32[264,128]{1,0:T(8,128)}, f32[264,128]{1,0:T(8,128)}, f32[4,128,128]{2,1,0:T(8,128)}, /*index=5*/f32[132,144,128]{2,1,0:T(8,128)S(1)}) custom-call(f32[128,128,128]{2,1,0:T(8,128)} %refs_0_.1), custom_call_target="tpu_custom_call" | custom-call | flops 20971520 | bytes 16777216 | tf_op jit(solution)/shard_map/pack/pallas_call | solution.py:423
  5.0 0.0 copy-start
  5.1 0.0 copy-start.1
  5.1 3.0 %collective-permute-start.2 = (f32[4,128,128]{2,1,0:T(8,128)}, f32[4,128,128]{2,1,0:T(8,128)S(1)}, u32[]{:S(2)}, u32[]{:S(2)}) collective-permute-start(f32[4,128,128]{2,1,0:T(8,128)} %get-tuple-element.18), channel_id=1, source_target_pairs={{0,1},{1,0},{2,3},{3,2},{4,5},{5,4},{6,7},{7,6},{8,9},{9,8},{10,11... | collective-permute-start | bytes 786440 | tf_op jit(solution)/shard_map/ppermute | solution.py:41
  8.1 1.6 %collective-permute-start = (f32[264,128]{1,0:T(8,128)}, f32[264,128]{1,0:T(8,128)S(1)}, u32[]{:S(2)}, u32[]{:S(2)}) collective-permute-start(f32[264,128]{1,0:T(8,128)} %get-tuple-element.16), channel_id=1, source_target_pairs={{0,8},{8,16},{16,24},{24,0},{1,9},{9,17},{17,25},{25,1},{2,10},{10... | collective-permute-start | bytes 405512 | tf_op jit(solution)/shard_map/ppermute | solution.py:34
  9.7 2.2 %collective-permute-start.1 = (f32[264,128]{1,0:T(8,128)}, f32[264,128]{1,0:T(8,128)S(1)}, u32[]{:S(2)}, u32[]{:S(2)}) collective-permute-start(f32[264,128]{1,0:T(8,128)} %get-tuple-element.17), channel_id=1, source_target_pairs={{8,0},{16,8},{24,16},{0,24},{9,1},{17,9},{25,17},{1,25},{10,2},{18... | collective-permute-start | bytes 405512 | tf_op jit(solution)/shard_map/ppermute | solution.py:34
  11.9 0.0 collective-permute-start.3
  11.9 1.7 %collective-permute-start.4 = (f32[2,128,128]{2,1,0:T(8,128)}, f32[2,128,128]{2,1,0:T(8,128)S(1)}, u32[]{:S(2)}, u32[]{:S(2)}) collective-permute-start(f32[2,128,128]{2,1,0:T(8,128)} %get-tuple-element.20.refs_8_.refs_6_), channel_id=1, source_target_pairs={{2,0},{4,2},{6,4},{0,6},{3,1},{5,3},{7,5},{1,7},{10,8},{12,10},{14... | collective-permute-start | bytes 393224 | tf_op jit(solution)/shard_map/ppermute | solution.py:34
  13.7 0.0 copy-done.2
  13.7 3.7 %weights.1 = (f32[128,64,128]{2,1,0:T(8,128)S(1)}, f32[64,128]{1,0:T(8,128)S(1)}) custom-call(f32[4]{0:T(128)S(1)} %copy-done.2, f32[132,144,128]{2,1,0:T(8,128)S(1)} %get-tuple-element.13.cells.refs_0_), custom_call_target="tpu_custom_call" | custom-call | flops 18874368 | bytes 8388608 | tf_op jit(solution)/shard_map/weights/pallas_call | solution.py:448
  17.4 0.0 collective-permute-done.3.refs_6_.refs_4_
  17.4 0.0 collective-permute-done.4.refs_7_.refs_5_
  17.4 0.0 collective-permute-done.refs_3_.refs_1_
  17.5 0.1 collective-permute-done.1.refs_4_.refs_2_
  17.6 0.0 collective-permute-done.2.refs_5_.refs_3_
  17.6 0.0 copy-done.3
  17.6 0.0 copy-done.4
  17.6 0.0 copy-done
  17.6 0.0 copy-done.1
  17.6 7.2 %shade.1 = f32[4,64,128]{2,1,0:T(8,128)S(1)} custom-call(f32[4]{0:T(128)S(1)} %copy-done.2, f32[3]{0:T(128)S(1)} %copy-done.3, f32[3]{0:T(128)S(1)} %copy-done.4, f32[132,144,128]{2,1,0:T(8,128)S(1)} %get-tuple-element.13.cells.refs_0_, f32[128,64,128]{2,1,0:T(8,128)S(1)} %get-tuple-element.14.refs_1_, f32[64,128]{1,0:T(8,128)S(1)} %get-tuple-element.15.refs_2_, ...), custom_call_target="tpu_custom_call" | custom-call | flops 41943040 | bytes 8388608 | tf_op jit(solution)/shard_map/shade/pallas_call | solution.py:477
  24.8 0.6 %collective-permute-start.5 = (f32[4,64,128]{2,1,0:T(8,128)S(1)}, f32[4,64,128]{2,1,0:T(8,128)S(1)}, u32[]{:S(2)}, u32[]{:S(2)}) collective-permute-start(f32[4,64,128]{2,1,0:T(8,128)S(1)} %shade.1), channel_id=1, source_target_pairs={{0,1},{1,0},{2,3},{3,2},{4,5},{5,4},{6,7},{7,6},{8,9},{9,8},{10,11... | collective-permute-start | bytes 393224 | tf_op jit(solution)/shard_map/ppermute | solution.py:488
  25.4 11.6 %fused.1 = f32[4,64,128]{2,1,0:T(8,128)S(1)} custom-call(f32[4]{0:T(128)S(1)} %copy-done.2, f32[3]{0:T(128)S(1)} %copy-done.3, f32[3]{0:T(128)S(1)} %copy-done.4, f32[128,128,128]{2,1,0:T(8,128)} %refs_0_.1, f32[264,128]{1,0:T(8,128)S(1)} %collective-permute-done.refs_3_.refs_1_, f32[264,128]{1,0:T(8,128)S(1)} %collective-permute-done.1.refs_4_.refs_2_, ...), custom_call_target="tpu_custom_call" | custom-call | flops 41943040 | bytes 8388608 | tf_op jit(solution)/shard_map/fused/pallas_call | solution.py:477
  36.9 0.0 collective-permute-done.5
  37.0 0.7 %add_select_fusion = f32[4,64,128]{2,1,0:T(8,128)} fusion(f32[4,64,128]{2,1,0:T(8,128)S(1)} %fused.1, f32[4,64,128]{2,1,0:T(8,128)S(1)} %collective-permute-done.5, f32[64,128]{1,0:T(8,128)S(1)} %get-tuple-element.22, f32[64,128]{1,0:T(8,128)S(1)} %get-tuple-element.23, f32[64,128]{1,0:T(8,128)S(1)} %get-tuple-element.21, pred[4]{0:T(512)(128)(4,1)S(1)} %iota_compare_fusion), kind=kLoop, calls=%fused_computation | loop fusion | flops 131072 | bytes 491524 | tf_op jit(solution)/shard_map/jit(_where)/select_n | solution.py:499
  (2 shorter events, 0.0 us)
Async XLA Ops:
  0.0 13.7 %copy-start.2 = (f32[4]{0:T(128)S(1)}, f32[4]{0:T(128)}, u32[]{:S(2)}) copy-start(f32[4]{0:T(128)} %peaks.5) | copy-start | bytes 52
  0.0 17.6 %copy-start.3 = (f32[3]{0:T(128)S(1)}, f32[3]{0:T(128)}, u32[]{:S(2)}) copy-start(f32[3]{0:T(128)} %tint.3) | copy-start | bytes 40
  0.0 17.6 %copy-start.4 = (f32[3]{0:T(128)S(1)}, f32[3]{0:T(128)}, u32[]{:S(2)}) copy-start(f32[3]{0:T(128)} %light.3) | copy-start | bytes 40
  5.0 12.5 %copy-start = (f32[2,128,128]{2,1,0:T(8,128)S(1)}, f32[2,128,128]{2,1,0:T(8,128)}, u32[]{:S(2)}) copy-start(f32[2,128,128]{2,1,0:T(8,128)} %get-tuple-element.20.refs_8_.refs_6_) | copy-start | bytes 393220
  5.1 12.5 %copy-start.1 = (f32[2,128,128]{2,1,0:T(8,128)S(1)}, f32[2,128,128]{2,1,0:T(8,128)}, u32[]{:S(2)}) copy-start(f32[2,128,128]{2,1,0:T(8,128)} %get-tuple-element.19.refs_9_.refs_7_) | copy-start | bytes 393220
  5.1 12.5 %collective-permute-start.2 = (f32[4,128,128]{2,1,0:T(8,128)}, f32[4,128,128]{2,1,0:T(8,128)S(1)}, u32[]{:S(2)}, u32[]{:S(2)}) collective-permute-start(f32[4,128,128]{2,1,0:T(8,128)} %get-tuple-element.18), channel_id=1, source_target_pairs={{0,1},{1,0},{2,3},{3,2},{4,5},{5,4},{6,7},{7,6},{8,9},{9,8},{10,11... | collective-permute-start | bytes 786440 | tf_op jit(solution)/shard_map/ppermute | solution.py:41
  8.1 9.3 %collective-permute-start = (f32[264,128]{1,0:T(8,128)}, f32[264,128]{1,0:T(8,128)S(1)}, u32[]{:S(2)}, u32[]{:S(2)}) collective-permute-start(f32[264,128]{1,0:T(8,128)} %get-tuple-element.16), channel_id=1, source_target_pairs={{0,8},{8,16},{16,24},{24,0},{1,9},{9,17},{17,25},{25,1},{2,10},{10... | collective-permute-start | bytes 405512 | tf_op jit(solution)/shard_map/ppermute | solution.py:34
  9.7 7.9 %collective-permute-start.1 = (f32[264,128]{1,0:T(8,128)}, f32[264,128]{1,0:T(8,128)S(1)}, u32[]{:S(2)}, u32[]{:S(2)}) collective-permute-start(f32[264,128]{1,0:T(8,128)} %get-tuple-element.17), channel_id=1, source_target_pairs={{8,0},{16,8},{24,16},{0,24},{9,1},{17,9},{25,17},{1,25},{10,2},{18... | collective-permute-start | bytes 405512 | tf_op jit(solution)/shard_map/ppermute | solution.py:34
  11.9 5.5 %collective-permute-start.3 = (f32[2,128,128]{2,1,0:T(8,128)}, f32[2,128,128]{2,1,0:T(8,128)S(1)}, u32[]{:S(2)}, u32[]{:S(2)}) collective-permute-start(f32[2,128,128]{2,1,0:T(8,128)} %get-tuple-element.19.refs_9_.refs_7_), channel_id=1, source_target_pairs={{0,2},{2,4},{4,6},{6,0},{1,3},{3,5},{5,7},{7,1},{8,10},{10,12},{12... | collective-permute-start | bytes 393224 | tf_op jit(solution)/shard_map/ppermute | solution.py:34
  11.9 5.5 %collective-permute-start.4 = (f32[2,128,128]{2,1,0:T(8,128)}, f32[2,128,128]{2,1,0:T(8,128)S(1)}, u32[]{:S(2)}, u32[]{:S(2)}) collective-permute-start(f32[2,128,128]{2,1,0:T(8,128)} %get-tuple-element.20.refs_8_.refs_6_), channel_id=1, source_target_pairs={{2,0},{4,2},{6,4},{0,6},{3,1},{5,3},{7,5},{1,7},{10,8},{12,10},{14... | collective-permute-start | bytes 393224 | tf_op jit(solution)/shard_map/ppermute | solution.py:34
  24.8 12.1 %collective-permute-start.5 = (f32[4,64,128]{2,1,0:T(8,128)S(1)}, f32[4,64,128]{2,1,0:T(8,128)S(1)}, u32[]{:S(2)}, u32[]{:S(2)}) collective-permute-start(f32[4,64,128]{2,1,0:T(8,128)S(1)} %shade.1), channel_id=1, source_target_pairs={{0,1},{1,0},{2,3},{3,2},{4,5},{5,4},{6,7},{7,6},{8,9},{9,8},{10,11... | collective-permute-start | bytes 393224 | tf_op jit(solution)/shard_map/ppermute | solution.py:488

commit v3 on v2

--- a/solution.py
+++ b/solution.py
@@ -423,11 +423,11 @@
     low, high, x_first, x_last, z_own, cells_in = pl.pallas_call(
         pack_kernel,
         out_shape=(
-            shape((depth // 64, rows, lanes), F32),
-            shape((depth // 64, rows, lanes), F32),
-            shape((HALO * depth + PAD, lanes), F32),
-            shape((HALO * depth + PAD, lanes), F32),
-            shape((2 * HALO, rows, lanes), F32),
+            pltpu.VMEM((depth // 64, rows, lanes), F32),
+            pltpu.VMEM((depth // 64, rows, lanes), F32),
+            pltpu.VMEM((HALO * depth + PAD, lanes), F32),
+            pltpu.VMEM((HALO * depth + PAD, lanes), F32),
+            pltpu.VMEM((2 * HALO, rows, lanes), F32),
             pltpu.VMEM(padded, F32),
         ),
         in_specs=[HBM],

time: 37.8 us -> 37.3 us (0.987)
    pallas_call x1, Pallas kernels: 5.03 us -> 4.25 us  [body(): pl.pallas_call(pack_kernel, out_shape=(pltpu.VMEM((depth // 64, rows, lan...]
    pallas_call x2, Pallas kernels: 18.8 us -> 19.3 us  [body(): pl.pallas_call(functools.partial(shade_kernel if ready else fused_kernel,...]
  transfers between devices with their start and end apart: 6 -> 6, of which waited for: 1 -> 0; matrix products, arithmetic and copies ran while one was open for 0% -> 0% of each run, Pallas kernels for 41% -> 41%
where the time goes in v3:
time: 37.3 us; the launch traced here: 37.2 us
  Pallas kernels  27.3 us (73%)
  starting transfers between devices  9.03 us (24%)
  other arithmetic  0.75 us (2%)
    pallas_call x2, Pallas kernels, body(): pl.pallas_call(functools.partial(shade_kernel if ready else fused_kernel,...  19.3 us
    pallas_call x1, Pallas kernels, body(): pl.pallas_call(pack_kernel, out_shape=(pltpu.VMEM((depth // 64, rows, lan...  4.25 us
    ppermute x2, starting transfers between devices, exchanged(): lax.ppermute(first, axis, backward)  3.99 us
    pallas_call x1, Pallas kernels, body(): pl.pallas_call(functools.partial(weight_kernel, scale, 1, count, part), o...  3.74 us
    ppermute x1, starting transfers between devices, exchanged_both(): return (lax.ppermute(both, axis, [(0, 1), (1, 0)]), width, 0)  3.03 us
    ppermute x2, starting transfers between devices, exchanged(): lax.ppermute(last, axis, forward)  1.58 us
  transfers between devices with their start and end apart: 6, of which 0 were waited for; matrix products, arithmetic and copies ran while one was open for 0% of the time, Pallas kernels for 41%

profile of v3, /device:TPU:0, one launch (start us, length us, event | category | flops | bytes accessed | tf_op | source)
XLA Modules:
  0.0 37.2 jit_solution(13411210527271790884)
XLA Ops:
  0.0 0.0 copy-start
  0.0 0.0 copy-start.1
  0.0 0.0 copy-start.2
  0.0 4.3 %pack.1 = (f32[2,128,128]{2,1,0:T(8,128)S(1)}, f32[2,128,128]{2,1,0:T(8,128)S(1)}, f32[264,128]{1,0:T(8,128)S(1)}, f32[264,128]{1,0:T(8,128)S(1)}, f32[4,128,128...) custom-call(f32[128,128,128]{2,1,0:T(8,128)} %refs_0_.1), custom_call_target="tpu_custom_call" | custom-call | flops 20971520 | bytes 16777216 | tf_op jit(solution)/shard_map/pack/pallas_call | solution.py:423
  4.3 3.0 %collective-permute-start.2 = (f32[4,128,128]{2,1,0:T(8,128)S(1)}, f32[4,128,128]{2,1,0:T(8,128)S(1)}, u32[]{:S(2)}, u32[]{:S(2)}) collective-permute-start(f32[4,128,128]{2,1,0:T(8,128)S(1)} %get-tuple-element.18), channel_id=1, source_target_pairs={{0,1},{1,0},{2,3},{3,2},{4,5},{5,4},{6,7},{7,6},{8,9},{9,8},{10,11... | collective-permute-start | bytes 786440 | tf_op jit(solution)/shard_map/ppermute | solution.py:41
  7.3 1.6 %collective-permute-start = (f32[264,128]{1,0:T(8,128)S(1)}, f32[264,128]{1,0:T(8,128)S(1)}, u32[]{:S(2)}, u32[]{:S(2)}) collective-permute-start(f32[264,128]{1,0:T(8,128)S(1)} %get-tuple-element.16), channel_id=1, source_target_pairs={{0,8},{8,16},{16,24},{24,0},{1,9},{9,17},{17,25},{25,1},{2,10},{10... | collective-permute-start | bytes 405512 | tf_op jit(solution)/shard_map/ppermute | solution.py:34
  8.9 2.2 %collective-permute-start.1 = (f32[264,128]{1,0:T(8,128)S(1)}, f32[264,128]{1,0:T(8,128)S(1)}, u32[]{:S(2)}, u32[]{:S(2)}) collective-permute-start(f32[264,128]{1,0:T(8,128)S(1)} %get-tuple-element.17), channel_id=1, source_target_pairs={{8,0},{16,8},{24,16},{0,24},{9,1},{17,9},{25,17},{1,25},{10,2},{18... | collective-permute-start | bytes 405512 | tf_op jit(solution)/shard_map/ppermute | solution.py:34
  11.1 0.0 collective-permute-start.3
  11.1 1.7 %collective-permute-start.4 = (f32[2,128,128]{2,1,0:T(8,128)S(1)}, f32[2,128,128]{2,1,0:T(8,128)S(1)}, u32[]{:S(2)}, u32[]{:S(2)}) collective-permute-start(f32[2,128,128]{2,1,0:T(8,128)S(1)} %get-tuple-element.20.refs_8_.refs_6_), channel_id=1, source_target_pairs={{2,0},{4,2},{6,4},{0,6},{3,1},{5,3},{7,5},{1,7},{10,8},{12,10},{14... | collective-permute-start | bytes 393224 | tf_op jit(solution)/shard_map/ppermute | solution.py:34
  12.9 0.0 copy-done
  12.9 3.7 %weights.1 = (f32[128,64,128]{2,1,0:T(8,128)S(1)}, f32[64,128]{1,0:T(8,128)S(1)}) custom-call(f32[4]{0:T(128)S(1)} %copy-done, f32[132,144,128]{2,1,0:T(8,128)S(1)} %get-tuple-element.13.cells.refs_0_), custom_call_target="tpu_custom_call" | custom-call | flops 18874368 | bytes 8388608 | tf_op jit(solution)/shard_map/weights/pallas_call | solution.py:448
  16.6 0.0 collective-permute-done.3.refs_6_.refs_4_
  16.6 0.0 collective-permute-done.4.refs_7_.refs_5_
  16.6 0.0 collective-permute-done.refs_3_.refs_1_
  16.7 0.0 collective-permute-done.1.refs_4_.refs_2_
  16.7 0.0 collective-permute-done.2.refs_5_.refs_3_
  16.7 0.0 copy-done.1
  16.7 0.0 copy-done.2
  16.7 7.7 %shade.1 = f32[4,64,128]{2,1,0:T(8,128)S(1)} custom-call(f32[4]{0:T(128)S(1)} %copy-done, f32[3]{0:T(128)S(1)} %copy-done.1, f32[3]{0:T(128)S(1)} %copy-done.2, f32[132,144,128]{2,1,0:T(8,128)S(1)} %get-tuple-element.13.cells.refs_0_, f32[128,64,128]{2,1,0:T(8,128)S(1)} %get-tuple-element.14.refs_1_, f32[64,128]{1,0:T(8,128)S(1)} %get-tuple-element.15.refs_2_, ...), custom_call_target="tpu_custom_call" | custom-call | flops 41943040 | bytes 8388608 | tf_op jit(solution)/shard_map/shade/pallas_call | solution.py:477
  24.4 0.4 %collective-permute-start.5 = (f32[4,64,128]{2,1,0:T(8,128)S(1)}, f32[4,64,128]{2,1,0:T(8,128)S(1)}, u32[]{:S(2)}, u32[]{:S(2)}) collective-permute-start(f32[4,64,128]{2,1,0:T(8,128)S(1)} %shade.1), channel_id=1, source_target_pairs={{0,1},{1,0},{2,3},{3,2},{4,5},{5,4},{6,7},{7,6},{8,9},{9,8},{10,11... | collective-permute-start | bytes 393224 | tf_op jit(solution)/shard_map/ppermute | solution.py:488
  24.9 11.6 %fused.1 = f32[4,64,128]{2,1,0:T(8,128)S(1)} custom-call(f32[4]{0:T(128)S(1)} %copy-done, f32[3]{0:T(128)S(1)} %copy-done.1, f32[3]{0:T(128)S(1)} %copy-done.2, f32[128,128,128]{2,1,0:T(8,128)} %refs_0_.1, f32[264,128]{1,0:T(8,128)S(1)} %collective-permute-done.refs_3_.refs_1_, f32[264,128]{1,0:T(8,128)S(1)} %collective-permute-done.1.refs_4_.refs_2_, ...), custom_call_target="tpu_custom_call" | custom-call | flops 41943040 | bytes 8388608 | tf_op jit(solution)/shard_map/fused/pallas_call | solution.py:477
  36.4 0.0 collective-permute-done.5
  36.5 0.7 %add_select_fusion = f32[4,64,128]{2,1,0:T(8,128)} fusion(f32[4,64,128]{2,1,0:T(8,128)S(1)} %fused.1, f32[4,64,128]{2,1,0:T(8,128)S(1)} %collective-permute-done.5, f32[64,128]{1,0:T(8,128)S(1)} %get-tuple-element.22, f32[64,128]{1,0:T(8,128)S(1)} %get-tuple-element.23, f32[64,128]{1,0:T(8,128)S(1)} %get-tuple-element.21, pred[4]{0:T(512)(128)(4,1)S(1)} %iota_compare_fusion), kind=kLoop, calls=%fused_computation | loop fusion | flops 131072 | bytes 491524 | tf_op jit(solution)/shard_map/jit(_where)/select_n | solution.py:499
  (2 shorter events, 0.0 us)
Async XLA Ops:
  0.0 12.9 %copy-start = (f32[4]{0:T(128)S(1)}, f32[4]{0:T(128)}, u32[]{:S(2)}) copy-start(f32[4]{0:T(128)} %peaks.5) | copy-start | bytes 52
  0.0 16.7 %copy-start.1 = (f32[3]{0:T(128)S(1)}, f32[3]{0:T(128)}, u32[]{:S(2)}) copy-start(f32[3]{0:T(128)} %tint.3) | copy-start | bytes 40
  0.0 16.7 %copy-start.2 = (f32[3]{0:T(128)S(1)}, f32[3]{0:T(128)}, u32[]{:S(2)}) copy-start(f32[3]{0:T(128)} %light.3) | copy-start | bytes 40
  4.3 12.4 %collective-permute-start.2 = (f32[4,128,128]{2,1,0:T(8,128)S(1)}, f32[4,128,128]{2,1,0:T(8,128)S(1)}, u32[]{:S(2)}, u32[]{:S(2)}) collective-permute-start(f32[4,128,128]{2,1,0:T(8,128)S(1)} %get-tuple-element.18), channel_id=1, source_target_pairs={{0,1},{1,0},{2,3},{3,2},{4,5},{5,4},{6,7},{7,6},{8,9},{9,8},{10,11... | collective-permute-start | bytes 786440 | tf_op jit(solution)/shard_map/ppermute | solution.py:41
  7.3 9.3 %collective-permute-start = (f32[264,128]{1,0:T(8,128)S(1)}, f32[264,128]{1,0:T(8,128)S(1)}, u32[]{:S(2)}, u32[]{:S(2)}) collective-permute-start(f32[264,128]{1,0:T(8,128)S(1)} %get-tuple-element.16), channel_id=1, source_target_pairs={{0,8},{8,16},{16,24},{24,0},{1,9},{9,17},{17,25},{25,1},{2,10},{10... | collective-permute-start | bytes 405512 | tf_op jit(solution)/shard_map/ppermute | solution.py:34
  8.9 7.8 %collective-permute-start.1 = (f32[264,128]{1,0:T(8,128)S(1)}, f32[264,128]{1,0:T(8,128)S(1)}, u32[]{:S(2)}, u32[]{:S(2)}) collective-permute-start(f32[264,128]{1,0:T(8,128)S(1)} %get-tuple-element.17), channel_id=1, source_target_pairs={{8,0},{16,8},{24,16},{0,24},{9,1},{17,9},{25,17},{1,25},{10,2},{18... | collective-permute-start | bytes 405512 | tf_op jit(solution)/shard_map/ppermute | solution.py:34
  11.1 5.5 %collective-permute-start.3 = (f32[2,128,128]{2,1,0:T(8,128)S(1)}, f32[2,128,128]{2,1,0:T(8,128)S(1)}, u32[]{:S(2)}, u32[]{:S(2)}) collective-permute-start(f32[2,128,128]{2,1,0:T(8,128)S(1)} %get-tuple-element.19.refs_9_.refs_7_), channel_id=1, source_target_pairs={{0,2},{2,4},{4,6},{6,0},{1,3},{3,5},{5,7},{7,1},{8,10},{10,12},{12... | collective-permute-start | bytes 393224 | tf_op jit(solution)/shard_map/ppermute | solution.py:34
  11.1 5.5 %collective-permute-start.4 = (f32[2,128,128]{2,1,0:T(8,128)S(1)}, f32[2,128,128]{2,1,0:T(8,128)S(1)}, u32[]{:S(2)}, u32[]{:S(2)}) collective-permute-start(f32[2,128,128]{2,1,0:T(8,128)S(1)} %get-tuple-element.20.refs_8_.refs_6_), channel_id=1, source_target_pairs={{2,0},{4,2},{6,4},{0,6},{3,1},{5,3},{7,5},{1,7},{10,8},{12,10},{14... | collective-permute-start | bytes 393224 | tf_op jit(solution)/shard_map/ppermute | solution.py:34
  24.4 12.0 %collective-permute-start.5 = (f32[4,64,128]{2,1,0:T(8,128)S(1)}, f32[4,64,128]{2,1,0:T(8,128)S(1)}, u32[]{:S(2)}, u32[]{:S(2)}) collective-permute-start(f32[4,64,128]{2,1,0:T(8,128)S(1)} %shade.1), channel_id=1, source_target_pairs={{0,1},{1,0},{2,3},{3,2},{4,5},{5,4},{6,7},{7,6},{8,9},{9,8},{10,11... | collective-permute-start | bytes 393224 | tf_op jit(solution)/shard_map/ppermute | solution.py:488

commit v4 on v3

--- a/solution.py
+++ b/solution.py
@@ -294,7 +294,8 @@
     begin = rows_of(shift, count, part)
     main = pl.ds(PAD, part)
 
-    for chunk in range(chunks):
+    soon = min(UNROLL // STEP + 1, chunks)
+    for chunk in range(soon):
         for copy in fetch(chunk):
             copy.start()
     lanes[...] = lane_matrix()
@@ -320,6 +321,9 @@
                 copy.wait()
         beside(chunk * STEP, number * STEP)
 
+    for chunk in range(soon, chunks):
+        for copy in fetch(chunk):
+            copy.start()
     arrive(0, 1)
     lane = lax.broadcasted_iota(jnp.int32, (group, LANES), 1)
     rim = (lane < HALO) | (lane >= LANES - HALO)

time: 37.3 us -> 37.3 us (level)
  no operation moved by 1% of the time
where the time goes in v4:
time: 37.3 us; the launch traced here: 37.2 us
  Pallas kernels  27.3 us (73%)
  starting transfers between devices  9.03 us (24%)
  other arithmetic  0.75 us (2%)
    pallas_call x2, Pallas kernels, body(): pl.pallas_call(functools.partial(shade_kernel if ready else fused_kernel,...  19.3 us
    pallas_call x1, Pallas kernels, body(): pl.pallas_call(pack_kernel, out_shape=(pltpu.VMEM((depth // 64, rows, lan...  4.25 us
    ppermute x2, starting transfers between devices, exchanged(): lax.ppermute(first, axis, backward)  3.99 us
    pallas_call x1, Pallas kernels, body(): pl.pallas_call(functools.partial(weight_kernel, scale, 1, count, part), o...  3.74 us
    ppermute x1, starting transfers between devices, exchanged_both(): return (lax.ppermute(both, axis, [(0, 1), (1, 0)]), width, 0)  3.03 us
    ppermute x2, starting transfers between devices, exchanged(): lax.ppermute(last, axis, forward)  1.58 us
  transfers between devices with their start and end apart: 6, of which 0 were waited for; matrix products, arithmetic and copies ran while one was open for 0% of the time, Pallas kernels for 41%

profile of v4, /device:TPU:0, one launch (start us, length us, event | category | flops | bytes accessed | tf_op | source)
XLA Modules:
  0.0 37.2 jit_solution(533642073906759134)
XLA Ops:
  0.0 0.0 copy-start
  0.0 0.0 copy-start.1
  0.0 0.0 copy-start.2
  0.0 4.3 %pack.1 = (f32[2,128,128]{2,1,0:T(8,128)S(1)}, f32[2,128,128]{2,1,0:T(8,128)S(1)}, f32[264,128]{1,0:T(8,128)S(1)}, f32[264,128]{1,0:T(8,128)S(1)}, f32[4,128,128...) custom-call(f32[128,128,128]{2,1,0:T(8,128)} %refs_0_.1), custom_call_target="tpu_custom_call" | custom-call | flops 20971520 | bytes 16777216 | tf_op jit(solution)/shard_map/pack/pallas_call | solution.py:427
  4.3 3.0 %collective-permute-start.2 = (f32[4,128,128]{2,1,0:T(8,128)S(1)}, f32[4,128,128]{2,1,0:T(8,128)S(1)}, u32[]{:S(2)}, u32[]{:S(2)}) collective-permute-start(f32[4,128,128]{2,1,0:T(8,128)S(1)} %get-tuple-element.18), channel_id=1, source_target_pairs={{0,1},{1,0},{2,3},{3,2},{4,5},{5,4},{6,7},{7,6},{8,9},{9,8},{10,11... | collective-permute-start | bytes 786440 | tf_op jit(solution)/shard_map/ppermute | solution.py:41
  7.3 1.6 %collective-permute-start = (f32[264,128]{1,0:T(8,128)S(1)}, f32[264,128]{1,0:T(8,128)S(1)}, u32[]{:S(2)}, u32[]{:S(2)}) collective-permute-start(f32[264,128]{1,0:T(8,128)S(1)} %get-tuple-element.16), channel_id=1, source_target_pairs={{0,8},{8,16},{16,24},{24,0},{1,9},{9,17},{17,25},{25,1},{2,10},{10... | collective-permute-start | bytes 405512 | tf_op jit(solution)/shard_map/ppermute | solution.py:34
  8.9 2.2 %collective-permute-start.1 = (f32[264,128]{1,0:T(8,128)S(1)}, f32[264,128]{1,0:T(8,128)S(1)}, u32[]{:S(2)}, u32[]{:S(2)}) collective-permute-start(f32[264,128]{1,0:T(8,128)S(1)} %get-tuple-element.17), channel_id=1, source_target_pairs={{8,0},{16,8},{24,16},{0,24},{9,1},{17,9},{25,17},{1,25},{10,2},{18... | collective-permute-start | bytes 405512 | tf_op jit(solution)/shard_map/ppermute | solution.py:34
  11.1 0.0 collective-permute-start.3
  11.1 1.7 %collective-permute-start.4 = (f32[2,128,128]{2,1,0:T(8,128)S(1)}, f32[2,128,128]{2,1,0:T(8,128)S(1)}, u32[]{:S(2)}, u32[]{:S(2)}) collective-permute-start(f32[2,128,128]{2,1,0:T(8,128)S(1)} %get-tuple-element.20.refs_8_.refs_6_), channel_id=1, source_target_pairs={{2,0},{4,2},{6,4},{0,6},{3,1},{5,3},{7,5},{1,7},{10,8},{12,10},{14... | collective-permute-start | bytes 393224 | tf_op jit(solution)/shard_map/ppermute | solution.py:34
  12.9 0.0 copy-done
  12.9 3.7 %weights.1 = (f32[128,64,128]{2,1,0:T(8,128)S(1)}, f32[64,128]{1,0:T(8,128)S(1)}) custom-call(f32[4]{0:T(128)S(1)} %copy-done, f32[132,144,128]{2,1,0:T(8,128)S(1)} %get-tuple-element.13.cells.refs_0_), custom_call_target="tpu_custom_call" | custom-call | flops 18874368 | bytes 8388608 | tf_op jit(solution)/shard_map/weights/pallas_call | solution.py:452
  16.6 0.0 collective-permute-done.3.refs_6_.refs_4_
  16.6 0.0 collective-permute-done.4.refs_7_.refs_5_
  16.6 0.0 collective-permute-done.refs_3_.refs_1_
  16.7 0.0 collective-permute-done.1.refs_4_.refs_2_
  16.7 0.0 collective-permute-done.2.refs_5_.refs_3_
  16.7 0.0 copy-done.1
  16.7 0.0 copy-done.2
  16.7 7.7 %shade.1 = f32[4,64,128]{2,1,0:T(8,128)S(1)} custom-call(f32[4]{0:T(128)S(1)} %copy-done, f32[3]{0:T(128)S(1)} %copy-done.1, f32[3]{0:T(128)S(1)} %copy-done.2, f32[132,144,128]{2,1,0:T(8,128)S(1)} %get-tuple-element.13.cells.refs_0_, f32[128,64,128]{2,1,0:T(8,128)S(1)} %get-tuple-element.14.refs_1_, f32[64,128]{1,0:T(8,128)S(1)} %get-tuple-element.15.refs_2_, ...), custom_call_target="tpu_custom_call" | custom-call | flops 41943040 | bytes 8388608 | tf_op jit(solution)/shard_map/shade/pallas_call | solution.py:481
  24.4 0.4 %collective-permute-start.5 = (f32[4,64,128]{2,1,0:T(8,128)S(1)}, f32[4,64,128]{2,1,0:T(8,128)S(1)}, u32[]{:S(2)}, u32[]{:S(2)}) collective-permute-start(f32[4,64,128]{2,1,0:T(8,128)S(1)} %shade.1), channel_id=1, source_target_pairs={{0,1},{1,0},{2,3},{3,2},{4,5},{5,4},{6,7},{7,6},{8,9},{9,8},{10,11... | collective-permute-start | bytes 393224 | tf_op jit(solution)/shard_map/ppermute | solution.py:492
  24.9 11.6 %fused.1 = f32[4,64,128]{2,1,0:T(8,128)S(1)} custom-call(f32[4]{0:T(128)S(1)} %copy-done, f32[3]{0:T(128)S(1)} %copy-done.1, f32[3]{0:T(128)S(1)} %copy-done.2, f32[128,128,128]{2,1,0:T(8,128)} %refs_0_.1, f32[264,128]{1,0:T(8,128)S(1)} %collective-permute-done.refs_3_.refs_1_, f32[264,128]{1,0:T(8,128)S(1)} %collective-permute-done.1.refs_4_.refs_2_, ...), custom_call_target="tpu_custom_call" | custom-call | flops 41943040 | bytes 8388608 | tf_op jit(solution)/shard_map/fused/pallas_call | solution.py:481
  36.4 0.0 collective-permute-done.5
  36.5 0.7 %add_select_fusion = f32[4,64,128]{2,1,0:T(8,128)} fusion(f32[4,64,128]{2,1,0:T(8,128)S(1)} %fused.1, f32[4,64,128]{2,1,0:T(8,128)S(1)} %collective-permute-done.5, f32[64,128]{1,0:T(8,128)S(1)} %get-tuple-element.22, f32[64,128]{1,0:T(8,128)S(1)} %get-tuple-element.23, f32[64,128]{1,0:T(8,128)S(1)} %get-tuple-element.21, pred[4]{0:T(512)(128)(4,1)S(1)} %iota_compare_fusion), kind=kLoop, calls=%fused_computation | loop fusion | flops 131072 | bytes 491524 | tf_op jit(solution)/shard_map/jit(_where)/select_n | solution.py:503
  (2 shorter events, 0.0 us)
Async XLA Ops:
  0.0 12.9 %copy-start = (f32[4]{0:T(128)S(1)}, f32[4]{0:T(128)}, u32[]{:S(2)}) copy-start(f32[4]{0:T(128)} %peaks.5) | copy-start | bytes 52
  0.0 16.7 %copy-start.1 = (f32[3]{0:T(128)S(1)}, f32[3]{0:T(128)}, u32[]{:S(2)}) copy-start(f32[3]{0:T(128)} %tint.3) | copy-start | bytes 40
  0.0 16.7 %copy-start.2 = (f32[3]{0:T(128)S(1)}, f32[3]{0:T(128)}, u32[]{:S(2)}) copy-start(f32[3]{0:T(128)} %light.3) | copy-start | bytes 40
  4.3 12.4 %collective-permute-start.2 = (f32[4,128,128]{2,1,0:T(8,128)S(1)}, f32[4,128,128]{2,1,0:T(8,128)S(1)}, u32[]{:S(2)}, u32[]{:S(2)}) collective-permute-start(f32[4,128,128]{2,1,0:T(8,128)S(1)} %get-tuple-element.18), channel_id=1, source_target_pairs={{0,1},{1,0},{2,3},{3,2},{4,5},{5,4},{6,7},{7,6},{8,9},{9,8},{10,11... | collective-permute-start | bytes 786440 | tf_op jit(solution)/shard_map/ppermute | solution.py:41
  7.3 9.3 %collective-permute-start = (f32[264,128]{1,0:T(8,128)S(1)}, f32[264,128]{1,0:T(8,128)S(1)}, u32[]{:S(2)}, u32[]{:S(2)}) collective-permute-start(f32[264,128]{1,0:T(8,128)S(1)} %get-tuple-element.16), channel_id=1, source_target_pairs={{0,8},{8,16},{16,24},{24,0},{1,9},{9,17},{17,25},{25,1},{2,10},{10... | collective-permute-start | bytes 405512 | tf_op jit(solution)/shard_map/ppermute | solution.py:34
  8.9 7.8 %collective-permute-start.1 = (f32[264,128]{1,0:T(8,128)S(1)}, f32[264,128]{1,0:T(8,128)S(1)}, u32[]{:S(2)}, u32[]{:S(2)}) collective-permute-start(f32[264,128]{1,0:T(8,128)S(1)} %get-tuple-element.17), channel_id=1, source_target_pairs={{8,0},{16,8},{24,16},{0,24},{9,1},{17,9},{25,17},{1,25},{10,2},{18... | collective-permute-start | bytes 405512 | tf_op jit(solution)/shard_map/ppermute | solution.py:34
  11.1 5.5 %collective-permute-start.3 = (f32[2,128,128]{2,1,0:T(8,128)S(1)}, f32[2,128,128]{2,1,0:T(8,128)S(1)}, u32[]{:S(2)}, u32[]{:S(2)}) collective-permute-start(f32[2,128,128]{2,1,0:T(8,128)S(1)} %get-tuple-element.19.refs_9_.refs_7_), channel_id=1, source_target_pairs={{0,2},{2,4},{4,6},{6,0},{1,3},{3,5},{5,7},{7,1},{8,10},{10,12},{12... | collective-permute-start | bytes 393224 | tf_op jit(solution)/shard_map/ppermute | solution.py:34
  11.1 5.5 %collective-permute-start.4 = (f32[2,128,128]{2,1,0:T(8,128)S(1)}, f32[2,128,128]{2,1,0:T(8,128)S(1)}, u32[]{:S(2)}, u32[]{:S(2)}) collective-permute-start(f32[2,128,128]{2,1,0:T(8,128)S(1)} %get-tuple-element.20.refs_8_.refs_6_), channel_id=1, source_target_pairs={{2,0},{4,2},{6,4},{0,6},{3,1},{5,3},{7,5},{1,7},{10,8},{12,10},{14... | collective-permute-start | bytes 393224 | tf_op jit(solution)/shard_map/ppermute | solution.py:34
  24.4 12.0 %collective-permute-start.5 = (f32[4,64,128]{2,1,0:T(8,128)S(1)}, f32[4,64,128]{2,1,0:T(8,128)S(1)}, u32[]{:S(2)}, u32[]{:S(2)}) collective-permute-start(f32[4,64,128]{2,1,0:T(8,128)S(1)} %shade.1), channel_id=1, source_target_pairs={{0,1},{1,0},{2,3},{3,2},{4,5},{5,4},{6,7},{7,6},{8,9},{9,8},{10,11... | collective-permute-start | bytes 393224 | tf_op jit(solution)/shard_map/ppermute | solution.py:492
